TPU v7x, 512 devices: a whole 4x8x8 slice. The times are simulated.
512 devices in a mesh: space: 64 (over z, y), rep: 8 (over x, core).
Axes of the slice: x: 4, y: 8, z: 8, core: 2. Of those that a mesh axis runs over, the one named last changes fastest.
Arguments:
- features: bfloat16 [8, 256, 96, 512], P('rep', 'space'), may hold values from -6 to 6
- occupancy: int32 [8, 256, 512], P('rep', 'space'), may hold values from 0 to 1, as said below
- neighbours: int32 [8, 256, 27], P('rep', 'space'), may hold values from 0 to 12, as said below
- owners: int32 [8, 256], P('rep', 'space'), may hold values from 0 to 63, as said below
- octslots: int32 [8, 256], P('rep', 'space'), may hold values from 0 to 15, as said below
- cotangent: bfloat16 [8, 128, 128, 512], P('rep', 'space'), may hold values from -0.046875 to 0.046875
- w_sub: bfloat16 [27, 96, 96], replicated, may hold values from -0.125 to 0.125
- w_down: bfloat16 [8, 128, 96], replicated, may hold values from -0.21875 to 0.21875
Outputs:
- coarse: bfloat16 [8, 128, 128, 512], P('rep', 'space')
- grad_sub: float32 [27, 96, 96], replicated
- grad_down: float32 [8, 128, 96], replicated
Inputs may be any that keep to these rules, and one draw needn't show every extreme that they name: `occupancy`: zero on every voxel of a slot past its device's count of active bricks; some device of each tile has all 4 slots active. `neighbours`: code n of offset (dx, dy, dz) is 12 or (dx + 1) * 4 + s, where s is the slot of an active brick on the space device dx away; the map has no bricks beyond its first and last space device; inactive slots have only 12. `owners`: the owner of a fine brick lies in the same aligned group of 8 space devices as the brick; no two bricks of one device have the same owner, so each owner receives at most one brick from each device. `octslots`: no two fine bricks with the same owner share a value.
All inputs are finite; a program needn't handle non-finite values.
Results may differ from a plain program's by a relative error of at most 0.0075.
Values may be sent and summed in bfloat16 or wider, within the bound.
A program may use at most 128 MiB of HBM per device.

v0:
```python
import functools

import jax
import jax.numpy as jnp
import numpy as np
from jax import lax
from jax.experimental import pallas as pl
from jax.experimental.pallas import tpu as pltpu
from jax.sharding import PartitionSpec as P

MESH = pl.DeviceIdType.MESH
NY = 8
PIECE = 48
QUARTER = NY * PIECE


class Place:
    def __init__(self, sizes):
        self.nz, self.nx = sizes
        space, rep = lax.axis_index("space"), lax.axis_index("rep")
        self.z, self.y = space // NY, space % NY
        self.x, self.core = rep // 2, rep % 2

    def across(self):
        return (self.z * NY + self.y, self.x * 2 + 1 - self.core)

    def along_x(self, k):
        return (self.z * NY + self.y, (self.x + k) % self.nx * 2 + self.core)

    def along_y(self, k):
        return (self.z * NY + (self.y + k) % NY, self.x * 2 + self.core)

    def along_z(self, k):
        return ((self.z + k) % self.nz * NY + self.y, self.x * 2 + self.core)

    def sum_partners(self):
        near = [self.across()]
        near += [self.along_x(k) for k in range(1, self.nx)]
        near += [self.along_y(k) for k in range(1, NY)]
        near += [self.along_z(k) for k in range(1, self.nz)]
        return near


def rows_at(start, count):
    return pl.ds(pl.multiple_of(start, 16), count)


def sum_scratch(sizes):
    nz, nx = sizes
    half = nx * QUARTER
    copies = 2 * nx + 2 * (nx - 1) + 2 * (NY - 1) + (nz - 1)
    return [
        pltpu.VMEM((half, 128), jnp.bfloat16),
        pltpu.VMEM((half, 128), jnp.bfloat16),
        pltpu.VMEM((nx - 1, QUARTER, 128), jnp.bfloat16),
        pltpu.VMEM((nx - 1, QUARTER, 128), jnp.bfloat16),
        pltpu.VMEM((QUARTER, 128), jnp.float32),
        pltpu.VMEM((QUARTER, 128), jnp.bfloat16),
        pltpu.VMEM((NY - 1, PIECE, 128), jnp.bfloat16),
        pltpu.VMEM((nz, PIECE, 128), jnp.bfloat16),
        pltpu.VMEM((2 * half, 128), jnp.bfloat16),
        pltpu.SemaphoreType.DMA((copies,)),
        pltpu.SemaphoreType.DMA((copies,)),
    ]


class GradSum:
    def __init__(self, place, scratch):
        self.place = place
        (self.core_out, self.core_in, self.x_out, self.x_in, self.mine, self.y_out,
         self.y_in, self.z_all, self.total, self.send_sem, self.recv_sem) = scratch
        self.used = 0
        self.sent = []

    def slot(self):
        self.used += 1
        return self.used - 1

    def send(self, slot, src, dst, device):
        copy = pltpu.make_async_remote_copy(
            src_ref=src, dst_ref=dst, send_sem=self.send_sem.at[slot],
            recv_sem=self.recv_sem.at[slot], device_id=device, device_id_type=MESH)
        copy.start()
        self.sent.append(copy)

    def arrive(self, slot, dst, device):
        pltpu.make_async_remote_copy(
            src_ref=dst, dst_ref=dst, send_sem=self.send_sem.at[slot],
            recv_sem=self.recv_sem.at[slot], device_id=device, device_id_type=MESH).wait_recv()

    def run(self, grads, meanwhile):
        at = self.place
        nx, nz = at.nx, at.nz
        half = nx * QUARTER
        x, y, z, core = at.x, at.y, at.z, at.core

        def quarter(i):
            return rows_at((x + 1 + i) % nx * QUARTER, QUARTER)

        core_slots = [self.slot() for _ in range(nx)]
        for i in range(nx):
            start = (1 - core) * half + (x + 1 + i) % nx * QUARTER
            self.core_out[quarter(i)] = grads[rows_at(start, QUARTER)].astype(BF16)
            self.send(core_slots[i], self.core_out.at[quarter(i)], self.core_in.at[quarter(i)],
                      at.across())
        x_slots = [self.slot() for _ in range(nx - 1)]
        for i in range(nx):
            self.arrive(core_slots[i], self.core_in.at[quarter(i)], at.across())
            start = core * half + (x + 1 + i) % nx * QUARTER
            pair = grads[rows_at(start, QUARTER)] + self.core_in[quarter(i)].astype(F32)
            if i < nx - 1:
                self.x_out[i] = pair.astype(BF16)
                self.send(x_slots[i], self.x_out.at[i], self.x_in.at[i], at.along_x(i + 1))
            else:
                self.mine[...] = pair
        for i in range(nx - 1):
            self.arrive(x_slots[i], self.x_in.at[i], at.along_x(-i - 1))
            self.mine[...] += self.x_in[i].astype(F32)
        self.y_out[...] = self.mine[...].astype(BF16)
        y_slots = [self.slot() for _ in range(NY - 1)]
        for k in range(1, NY):
            self.send(y_slots[k - 1], self.y_out.at[rows_at((y + k) % NY * PIECE, PIECE)],
                      self.y_in.at[k - 1], at.along_y(k))
        meanwhile()
        piece = self.mine[rows_at(y * PIECE, PIECE)]
        for k in range(1, NY):
            self.arrive(y_slots[k - 1], self.y_in.at[k - 1], at.along_y(-k))
            piece = piece + self.y_in[k - 1].astype(F32)
        self.z_all[z] = piece.astype(BF16)
        z_slots = [self.slot() for _ in range(nz - 1)]
        for k in range(1, nz):
            self.send(z_slots[k - 1], self.z_all.at[z], self.z_all.at[z], at.along_z(k))
        for k in range(1, nz):
            self.arrive(z_slots[k - 1], self.z_all.at[(z - k) % nz], at.along_z(-k))
        piece = self.z_all[0].astype(F32)
        for layer in range(1, nz):
            piece = piece + self.z_all[layer].astype(F32)
        base = core * half + x * QUARTER

        def piece_rows(k):
            return rows_at(base + (y + k) % NY * PIECE, PIECE)

        self.total[piece_rows(0)] = piece.astype(BF16)
        y_slots = [self.slot() for _ in range(NY - 1)]
        for k in range(1, NY):
            self.send(y_slots[k - 1], self.total.at[piece_rows(0)], self.total.at[piece_rows(0)],
                      at.along_y(k))
        for k in range(1, NY):
            self.arrive(y_slots[k - 1], self.total.at[piece_rows(-k)], at.along_y(-k))

        def quarter_of(which, k):
            return rows_at(which * half + (x + k) % nx * QUARTER, QUARTER)

        x_slots = [self.slot() for _ in range(nx - 1)]
        core_slots = [self.slot() for _ in range(nx)]
        own = self.total.at[quarter_of(core, 0)]
        for k in range(1, nx):
            self.send(x_slots[k - 1], own, own, at.along_x(k))
        self.send(core_slots[0], own, own, at.across())
        for k in range(1, nx):
            other = self.total.at[quarter_of(core, -k)]
            self.arrive(x_slots[k - 1], other, at.along_x(-k))
            self.send(core_slots[k], other, other, at.across())
        for k in range(nx):
            self.arrive(core_slots[k], self.total.at[quarter_of(1 - core, -k)], at.across())

    def finish(self):
        for copy in self.sent:
            copy.wait_send()

F32, BF16 = jnp.float32, jnp.bfloat16
NT = (((1,), (1,)), ((), ()))
NN = (((1,), (0,)), ((), ()))
TN = (((0,), (0,)), ((), ()))
BRICKS = 4
FINE = 96
COARSE = 128
TAPS = 9
SUB_ROWS = 3 * FINE
SUB_BLOCKS = 7
DOWN_ROWS = 2 * COARSE
DOWN_START = SUB_ROWS * SUB_BLOCKS
USED_ROWS = DOWN_START + 3 * DOWN_ROWS


def mul(a, b, dims=NN):
    return lax.dot_general(a, b, dims, preferred_element_type=F32)


def padding_matrix():
    out = np.zeros((9, 2, 8, 8, 2, 128), np.float32)
    sides = ([(7, 0)], [(i, i + 1) for i in range(8)], [(0, 9)])
    for layer_y in range(3):
        for layer_z in range(3):
            for y, to_y in sides[layer_y]:
                for z, to_z in sides[layer_z]:
                    for half in range(2):
                        out[3 * layer_y + layer_z, half, y, z, half, 10 * to_y + to_z] = 1
    return out.reshape(9 * 128, 256).astype(jnp.bfloat16)


def octant_matrix():
    out = np.zeros((8, 128, 8, 64), np.float32)
    for x in range(8):
        for y in range(8):
            for z in range(8):
                octant = x % 2 * 4 + y % 2 * 2 + z % 2
                out[x, 10 * (y + 1) + z + 1, octant, x // 2 * 16 + y // 2 * 4 + z // 2] = 1
    return out.reshape(1024, 512).astype(jnp.bfloat16)


def placing_matrix():
    out = np.zeros((8, 2, 64, 8, 8, 8), np.float32)
    for octant in range(8):
        for v in range(64):
            x, y, z = v // 16, v // 4 % 4, v % 4
            spot = (octant // 4 * 4 + x, octant // 2 % 2 * 4 + y, octant % 2 * 4 + z)
            out[(octant, slice(None), v) + spot] = 1
    return out.reshape(1024, 512).astype(jnp.bfloat16)


def low_lanes(shape):
    return lax.broadcasted_iota(jnp.int32, shape, len(shape) - 1) % 128 < 64


def packed(block):
    return jnp.where(low_lanes((64, 128)), block[:64], block[64:])


def chosen(labels, slot, table):
    hit = jnp.where(labels[0:1] == slot, 1.0, 0.0).astype(BF16)
    return hit * table


def kernel(sizes, neighbours, owners, octslots, features, occupancy, cotangent, w_sub, w_down,
           pad_m, oct_m, place_m, coarse, grad_sub, grad_down,
           source, upper, lower, gathered, edge, window, wide, occ_pad, active, act_oct, w_cat, w_pair,
           oct_pack, oct_out, oct_in, lab_out, lab_in, table, rep_out, rep_in, returned, ret_half,
           back, shifted, grads, place_in, pair_send, pair_recv, *sum_refs):
    at = Place(sizes)
    work = GradSum(at, sum_refs)
    nspace = at.nz * NY
    me = at.z * NY + at.y
    rep = at.x * 2 + at.core
    above, below = ((me + 1) % nspace, rep), ((me + nspace - 1) % nspace, rep)
    partners = at.sum_partners() + [above, below]
    barrier = pltpu.get_barrier_semaphore()
    for partner in partners:
        pl.semaphore_signal(barrier, inc=1, device_id=partner, device_id_type=MESH)

    def link(slot, src, dst, device):
        return pltpu.make_async_remote_copy(
            src_ref=src, dst_ref=dst, send_sem=pair_send.at[slot], recv_sem=pair_recv.at[slot],
            device_id=device, device_id_type=MESH)

    started = []

    def send(slot, src, dst, device):
        copy = link(slot, src, dst, device)
        copy.start()
        started.append(copy)

    occ = occupancy[...].astype(BF16)
    for j in range(BRICKS):
        source[j] = features[j] * occ[j:j + 1]
    source[BRICKS] = jnp.zeros((FINE, 512), BF16)
    upper[BRICKS] = jnp.zeros((FINE, 128), BF16)
    lower[BRICKS] = jnp.zeros((FINE, 128), BF16)
    owner_of = [owners[j] % NY for j in range(BRICKS)]

    def brick_for(member):
        found = BRICKS
        for j in range(BRICKS):
            found = jnp.where(owner_of[j] == member, j, found)
        return found

    for k in range(NY):
        member = (at.y + k) % NY
        label = -1
        for j in range(BRICKS):
            label = jnp.where(owner_of[j] == member, octslots[j], label)
        lab_out[k] = jnp.full((8, 128), label, jnp.int32)

    pl.semaphore_wait(barrier, len(partners))
    first, last = pl.ds(0, BRICKS), pl.ds(384, 128)
    send(0, source.at[first, :, last], lower.at[first], above)
    send(1, source.at[first, :, pl.ds(0, 128)], upper.at[first], below)
    for k in range(1, NY):
        send(1 + k, lab_out.at[k], lab_in.at[k], at.along_y(k))
    lab_in[0] = lab_out[0]

    spread = mul(cotangent[...].reshape(2 * COARSE, 512), place_m[...], NT)
    for s in range(2):
        for m in range(8):
            block = spread[s * COARSE:(s + 1) * COARSE, m * 128:(m + 1) * 128]
            table[8 * s + m] = packed(block).astype(BF16)
    for kx in range(3):
        w_cat[kx * FINE:(kx + 1) * FINE] = jnp.concatenate(
            [w_sub[TAPS * kx + t] for t in range(TAPS)], axis=1)
    for parity in range(2):
        w_pair[parity * COARSE:(parity + 1) * COARSE] = jnp.concatenate(
            [w_down[2 * pair + parity] for pair in range(4)], axis=1)
    center = pad_m[pl.ds(4 * 128, 128)]
    for p in range(4):
        occ_pad[:, p * 256:(p + 1) * 256] = mul(occ[:, p * 128:(p + 1) * 128], center)

    for k in range(NY):
        if k:
            link(1 + k, lab_out.at[k], lab_in.at[k], at.along_y(-k)).wait_recv()
        labels = lab_in[k]
        answer = chosen(labels, 0, table[0])
        for slot in range(1, 16):
            answer = answer + chosen(labels, slot, table[slot])
        if k:
            rep_out[k] = answer
            send(8 + k, rep_out.at[k], rep_in.at[k], at.along_y(-k))
        else:
            rep_in[0] = answer

    def put(j, block, position):
        for t in range(TAPS):
            shift = (t // 3 - 1) * 10 + t % 3 - 1
            rolled = pltpu.roll(block, (-shift) % 128, 1) if shift else block
            window[j, t * FINE:(t + 1) * FINE, position * 128:(position + 1) * 128] = rolled.astype(BF16)

    def own_planes(j, carry):
        for n in range(9):
            code = neighbours[j, 9 + n]
            which = jnp.clip(code - BRICKS, 0, BRICKS)
            for p in range(4):
                gathered[p * FINE:(p + 1) * FINE, n * 128:(n + 1) * 128] = (
                    source[which, :, p * 128:(p + 1) * 128])
        planes = mul(gathered[...], pad_m[...])
        for p in range(4):
            for half in range(2):
                put(j, planes[p * FINE:(p + 1) * FINE, half * 128:(half + 1) * 128], 2 * p + half + 1)
        return carry

    lax.fori_loop(0, BRICKS, own_planes, 0)

    link(0, source.at[first, :, last], lower.at[first], below).wait_recv()
    link(1, source.at[first, :, pl.ds(0, 128)], upper.at[first], above).wait_recv()

    def convolve(j, carry):
        for n in range(9):
            low, high = neighbours[j, n], neighbours[j, 18 + n]
            which_low = jnp.clip(low, 0, BRICKS)
            which_high = jnp.clip(high - 2 * BRICKS, 0, BRICKS)
            edge[:, n * 128:(n + 1) * 128] = jnp.where(
                low_lanes((FINE, 128)), upper[which_high], lower[which_low])
        planes = mul(edge[...], pad_m[...])
        put(j, planes[:, :128], 9)
        put(j, planes[:, 128:], 0)
        wide[...] = mul(w_cat[...], window[j])
        total = wide[0:FINE, 0:1024]
        total = total + wide[FINE:2 * FINE, 128:1152]
        total = total + wide[2 * FINE:3 * FINE, 256:1280]
        pre_act = total * occ_pad[pl.ds(j, 1)]
        active[rows_at(j * FINE, FINE)] = jnp.maximum(pre_act, 0.0).astype(BF16)
        return carry

    lax.fori_loop(0, BRICKS, convolve, 0)

    octants = mul(active[...], oct_m[...]).astype(BF16)
    for j in range(BRICKS):
        for pair in range(4):
            act_oct[pair * FINE:(pair + 1) * FINE, j * 128:(j + 1) * 128] = (
                octants[j * FINE:(j + 1) * FINE, pair * 128:(pair + 1) * 128])
    summed = mul(w_pair[...], act_oct[...])
    for j in range(BRICKS):
        even = summed[:COARSE, j * 128:(j + 1) * 128]
        odd = summed[COARSE:, j * 128:(j + 1) * 128]
        both = jnp.where(low_lanes((COARSE, 128)), even, odd)
        both = both + pltpu.roll(both, 64, 1)
        oct_pack[j] = packed(both).astype(BF16)
    oct_pack[BRICKS] = jnp.zeros((64, 128), BF16)
    for k in range(NY):
        block = oct_pack[brick_for((at.y + k) % NY)]
        if k:
            oct_out[k] = block
            send(15 + k, oct_out.at[k], oct_in.at[k], at.along_y(k))
        else:
            oct_in[0] = block

    for k in range(1, NY):
        link(8 + k, rep_out.at[k], rep_in.at[k], at.along_y(k)).wait_recv()
    low = low_lanes((64, 128))
    for j in range(BRICKS):
        block = rep_in[(owner_of[j] - at.y + NY) % NY].astype(F32)
        turned = pltpu.roll(block, 64, 1)
        returned[0:64, j * 128:(j + 1) * 128] = jnp.where(low, block, turned).astype(BF16)
        returned[64:128, j * 128:(j + 1) * 128] = jnp.where(low, turned, block).astype(BF16)
    whole = returned[...].astype(F32)
    low = low_lanes((COARSE, 512))
    ret_half[:COARSE] = jnp.where(low, whole, 0.0).astype(BF16)
    ret_half[COARSE:] = jnp.where(low, 0.0, whole).astype(BF16)
    down = mul(ret_half[...], act_oct[...], NT)
    for b in range(3):
        start = DOWN_START + b * DOWN_ROWS
        grads[start:start + DOWN_ROWS] = down[:, b * 128:(b + 1) * 128]
    grads[USED_ROWS:] = jnp.zeros((grads.shape[0] - USED_ROWS, 128), F32)
    low = low_lanes((FINE, 512))
    for pair in range(4):
        even = mul(w_down[2 * pair], returned[...], TN)
        odd = mul(w_down[2 * pair + 1], returned[...], TN)
        both = jnp.where(low, even, odd).astype(BF16)
        for j in range(BRICKS):
            back[j * FINE:(j + 1) * FINE, pair * 128:(pair + 1) * 128] = both[:, j * 128:(j + 1) * 128]

    shifted[...] = jnp.zeros(shifted.shape, BF16)

    def weight_gradient(j, carry):
        rows = rows_at(j * FINE, FINE)
        grad_act = mul(back[rows], oct_m[...], NT)
        grad_pre = jnp.where(active[rows].astype(F32) > 0, grad_act, 0.0).astype(BF16)
        for kx in range(3):
            shifted[kx * FINE:(kx + 1) * FINE, kx * 128:kx * 128 + 1024] = grad_pre
        part = mul(shifted[...], window[j], NT)

        @pl.when(j == 0)
        def _():
            for b in range(6):
                grads[b * SUB_ROWS:(b + 1) * SUB_ROWS] = part[:, b * 128:(b + 1) * 128]
            grads[6 * SUB_ROWS:7 * SUB_ROWS] = jnp.zeros((SUB_ROWS, 128), F32)
            grads[6 * SUB_ROWS:7 * SUB_ROWS, 0:96] = part[:, 768:864]

        @pl.when(j > 0)
        def _():
            for b in range(6):
                grads[b * SUB_ROWS:(b + 1) * SUB_ROWS] += part[:, b * 128:(b + 1) * 128]
            grads[6 * SUB_ROWS:7 * SUB_ROWS, 0:96] += part[:, 768:864]

        return carry

    lax.fori_loop(0, BRICKS, weight_gradient, 0)

    def place_octants():
        for k in range(1, NY):
            link(15 + k, oct_out.at[k], oct_in.at[k], at.along_y(-k)).wait_recv()
        low = low_lanes((64, 128))
        for slot in range(16):
            s, m = slot // 8, slot % 8
            block = chosen(lab_in[0], slot, oct_in[0])
            for k in range(1, NY):
                block = block + chosen(lab_in[k], slot, oct_in[k])
            block = block.astype(F32)
            lanes = slice(m * 128, (m + 1) * 128)
            place_in[s * 128:s * 128 + 64, lanes] = jnp.where(low, block, 0.0).astype(BF16)
            place_in[s * 128 + 64:s * 128 + 128, lanes] = jnp.where(low, 0.0, block).astype(BF16)
        result = mul(place_in[...], place_m[...]).astype(BF16)
        for s in range(2):
            coarse[s] = result[s * COARSE:(s + 1) * COARSE]

    work.run(grads, place_octants)

    def side_by_side(base, rows, block, start):
        b, offset = start // 128, start % 128
        left = work.total[base + b * block + rows.start:base + b * block + rows.stop].astype(F32)
        if offset:
            left = pltpu.roll(left, 128 - offset, 1)
        if offset > 32:
            right = work.total[base + (b + 1) * block + rows.start:
                               base + (b + 1) * block + rows.stop].astype(F32)
            right = pltpu.roll(right, 128 - offset, 1)
            lane = lax.broadcasted_iota(jnp.int32, left.shape, 1)
            left = jnp.where(lane < 128 - offset, left, right)
        return left[:, :FINE]

    for kx in range(3):
        for t in range(TAPS):
            rows = slice(kx * FINE, (kx + 1) * FINE)
            grad_sub[TAPS * kx + t] = side_by_side(0, rows, SUB_ROWS, t * FINE)
    for octant in range(8):
        rows = slice(octant % 2 * COARSE, (octant % 2 + 1) * COARSE)
        grad_down[octant] = side_by_side(DOWN_START, rows, DOWN_ROWS, octant // 2 * FINE)
    for copy in started:
        copy.wait_send()
    work.finish()


def per_device(sizes, features, occupancy, neighbours, owners, octslots, cotangent, w_sub, w_down):
    vmem = pl.BlockSpec(memory_space=pltpu.VMEM)
    smem = pl.BlockSpec(memory_space=pltpu.SMEM)
    v = pltpu.VMEM
    coarse, grad_sub, grad_down = pl.pallas_call(
        functools.partial(kernel, sizes),
        out_shape=(
            jax.ShapeDtypeStruct(cotangent.shape[1:], BF16),
            jax.ShapeDtypeStruct(w_sub.shape, F32),
            jax.ShapeDtypeStruct(w_down.shape, F32),
        ),
        in_specs=[smem] * 3 + [vmem] * 8,
        out_specs=(vmem, vmem, vmem),
        scratch_shapes=[
            v((BRICKS + 1, FINE, 512), BF16),
            v((BRICKS + 1, FINE, 128), BF16),
            v((BRICKS + 1, FINE, 128), BF16),
            v((4 * FINE, TAPS * 128), BF16),
            v((FINE, TAPS * 128), BF16),
            v((BRICKS, TAPS * FINE, 1280), BF16),
            v((3 * FINE, 1280), F32),
            v((BRICKS, 1024), F32),
            v((BRICKS * FINE, 1024), BF16),
            v((4 * FINE, BRICKS * 128), BF16),
            v((3 * FINE, TAPS * FINE), BF16),
            v((2 * COARSE, 4 * FINE), BF16),
            v((BRICKS + 1, 64, 128), BF16),
            v((NY, 64, 128), BF16),
            v((NY, 64, 128), BF16),
            v((NY, 8, 128), jnp.int32),
            v((NY, 8, 128), jnp.int32),
            v((16, 64, 128), BF16),
            v((NY, 64, 128), BF16),
            v((NY, 64, 128), BF16),
            v((COARSE, BRICKS * 128), BF16),
            v((2 * COARSE, BRICKS * 128), BF16),
            v((BRICKS * FINE, 512), BF16),
            v((3 * FINE, 1280), BF16),
            v((2 * sizes[1] * QUARTER, 128), F32),
            v((2 * COARSE, 1024), BF16),
            pltpu.SemaphoreType.DMA((2 + 3 * (NY - 1),)),
            pltpu.SemaphoreType.DMA((2 + 3 * (NY - 1),)),
        ] + sum_scratch(sizes),
        compiler_params=pltpu.CompilerParams(
            collective_id=0, has_side_effects=True, vmem_limit_bytes=56 * 2**20
        ),
    )(neighbours[0], owners[0], octslots[0], features[0], occupancy[0], cotangent[0], w_sub, w_down,
      jnp.asarray(padding_matrix()), jnp.asarray(octant_matrix()), jnp.asarray(placing_matrix()))
    return coarse[None], grad_sub, grad_down


def solution(mesh):
    sizes = (mesh.shape["space"] // NY, mesh.shape["rep"] // 2)
    return jax.shard_map(
        functools.partial(per_device, sizes),
        mesh=mesh,
        in_specs=(
            P("rep", "space", None, None),
            P("rep", "space", None),
            P("rep", "space", None),
            P("rep", "space"),
            P("rep", "space"),
            P("rep", "space", None, None),
            P(),
            P(),
        ),
        out_specs=(P("rep", "space", None, None), P(), P()),
        check_vma=False,
    )
```

profile of v0, /device:TPU:1, one launch (start us, length us, event | category | flops | bytes accessed | tf_op | source)
XLA Modules:
  0.0 80.3 jit_solution(4620236294555086943)
XLA Ops:
  0.6 1.8 %copy.14.w_down = bf16[8,128,96]{2,1,0:T(8,128)(2,1)} copy(bf16[8,128,96]{1,2,0:T(8,128)(2,1)} %param.18) | data formatting | bytes 393216 | tf_op args[7]
  2.4 73.1 %shard_map.130 = (bf16[2,128,512]{2,1,0:T(8,128)(2,1)}, f32[27,96,96]{2,1,0:T(8,128)}, f32[8,128,96]{2,1,0:T(8,128)}) custom-call(s32[4,27]{1,0:T(4,128)} %bitcast.11, s32[4]{0:T(128)} %bitcast.12, s32[4]{0:T(128)} %bitcast.13, bf16[4,96,512]{2,1,0:T(8,128)(2,1)} %bitcast.7, s32[4,512]{1,0:T(4,128)} %bitcast.10, bf16[2,128,512]{2,1,0:T(8,128)(2,1)} %bitcast.8, ...), custom_call_target="tpu_custom_call" | custom-call | tf_op jit(solution)/shard_map/pallas_call | solution.py:485
  75.5 0.0 copy-start
  75.5 2.1 %copy.15 = f32[8,128,96]{1,2,0:T(8,128)} copy(f32[8,128,96]{2,1,0:T(8,128)} %get-tuple-element.11) | data formatting | bytes 786432
  77.6 1.7 %copy.18 = bf16[1,2,128,512]{3,2,1,0:T(8,128)(2,1)} copy(bf16[1,2,128,512]{3,2,1,0:T(8,128)(2,1)} %bitcast.9) | data formatting | bytes 524288
  79.2 0.0 copy-done
  79.2 1.1 %copy.19 = f32[27,96,96]{2,1,0:T(8,128)} copy(f32[27,96,96]{2,1,0:T(8,128)S(1)} %copy-done) | data formatting | bytes 1990656
Async XLA Ops:
  75.5 3.8 %copy-start = (f32[27,96,96]{2,1,0:T(8,128)S(1)}, f32[27,96,96]{2,1,0:T(8,128)}, u32[]{:S(2)}) copy-start(f32[27,96,96]{2,1,0:T(8,128)} %get-tuple-element.16) | copy-start | bytes 2985988
where the time goes:
time: 80.5 us; the launch traced here: 80.3 us
  Pallas kernels  73.1 us (91%)
  local copies, waits for them, and re-layouts  6.59 us (8%)
    pallas_call x1, Pallas kernels, per_device(): pl.pallas_call(functools.partial(kernel, sizes), out_shape=(jax.ShapeDtyp...  73.1 us
    unnamed x6, local copies, waits for them, and re-layouts  6.59 us

commit v1 on v0

v1 whole, which is shorter than its diff:
```python
import functools

import jax
import jax.numpy as jnp
import numpy as np
from jax import lax
from jax.experimental import pallas as pl
from jax.experimental.pallas import tpu as pltpu
from jax.sharding import PartitionSpec as P

MESH = pl.DeviceIdType.MESH
F32, BF16 = jnp.float32, jnp.bfloat16
NT = (((1,), (1,)), ((), ()))
NN = (((1,), (0,)), ((), ()))
TN = (((0,), (0,)), ((), ()))
NY = 8
BRICKS = 4
FINE = 96
COARSE = 128
TAPS = 9
PLANES = 640
SUB_ROWS = 3 * FINE
DOWN_ROWS = 4 * FINE
FIRST_BLOCKS = 4
LAST_BLOCKS = 3
FIRST_PIECE = 32
LAST_PIECE = 16
DOWN_START = FIRST_BLOCKS * SUB_ROWS


class Place:
    def __init__(self, sizes):
        self.nz, self.nx = sizes
        space, rep = lax.axis_index("space"), lax.axis_index("rep")
        self.z, self.y = space // NY, space % NY
        self.x, self.core = rep // 2, rep % 2

    def across(self):
        return (self.z * NY + self.y, self.x * 2 + 1 - self.core)

    def along_x(self, k):
        return (self.z * NY + self.y, (self.x + k) % self.nx * 2 + self.core)

    def along_y(self, k):
        return (self.z * NY + (self.y + k) % NY, self.x * 2 + self.core)

    def along_z(self, k):
        return ((self.z + k) % self.nz * NY + self.y, self.x * 2 + self.core)

    def sum_partners(self):
        near = [self.across()]
        near += [self.along_x(k) for k in range(1, self.nx)]
        near += [self.along_y(k) for k in range(1, NY)]
        near += [self.along_z(k) for k in range(1, self.nz)]
        return near


def rows_at(start, count):
    return pl.ds(pl.multiple_of(start, 16), count)


def sum_rows(sizes, piece):
    return 2 * sizes[1] * NY * piece


def sum_scratch(sizes, piece):
    nz, nx = sizes
    quarter = NY * piece
    half = nx * quarter
    copies = 2 * nx + 2 * (nx - 1) + 2 * (NY - 1) + (nz - 1)
    return [
        pltpu.VMEM((2 * half, 128), F32),
        pltpu.VMEM((half, 128), BF16),
        pltpu.VMEM((half, 128), BF16),
        pltpu.VMEM((nx - 1, quarter, 128), BF16),
        pltpu.VMEM((nx - 1, quarter, 128), BF16),
        pltpu.VMEM((quarter, 128), F32),
        pltpu.VMEM((quarter, 128), BF16),
        pltpu.VMEM((NY - 1, piece, 128), BF16),
        pltpu.VMEM((nz, piece, 128), BF16),
        pltpu.VMEM((2 * half, 128), BF16),
        pltpu.SemaphoreType.DMA((copies,)),
        pltpu.SemaphoreType.DMA((copies,)),
        pltpu.SemaphoreType.DMA((2 * nx,)),
    ]


class GradSum:
    def __init__(self, place, piece, scratch, result):
        self.place, self.piece, self.result = place, piece, result
        (self.grads, self.core_out, self.core_in, self.x_out, self.x_in, self.mine, self.y_out,
         self.y_in, self.z_all, self.total, self.send_sem, self.recv_sem, self.save_sem) = scratch
        self.used = 0
        self.sent = []
        self.saved = []

    def slots(self, count):
        self.used += count
        return range(self.used - count, self.used)

    def send(self, slot, src, dst, device):
        copy = pltpu.make_async_remote_copy(
            src_ref=src, dst_ref=dst, send_sem=self.send_sem.at[slot],
            recv_sem=self.recv_sem.at[slot], device_id=device, device_id_type=MESH)
        copy.start()
        self.sent.append(copy)

    def arrive(self, slot, dst, device):
        pltpu.make_async_remote_copy(
            src_ref=dst, dst_ref=dst, send_sem=self.send_sem.at[slot],
            recv_sem=self.recv_sem.at[slot], device_id=device, device_id_type=MESH).wait_recv()

    def save(self, rows):
        copy = pltpu.make_async_copy(
            self.total.at[rows], self.result.at[rows], self.save_sem.at[len(self.saved)])
        copy.start()
        self.saved.append(copy)

    def phases(self):
        at, piece, grads = self.place, self.piece, self.grads
        nx, nz = at.nx, at.nz
        quarter = NY * piece
        half = nx * quarter
        x, y, z, core = at.x, at.y, at.z, at.core

        def part(i):
            return rows_at((x + 1 + i) % nx * quarter, quarter)

        core_slots = self.slots(nx)
        for i in range(nx):
            start = (1 - core) * half + (x + 1 + i) % nx * quarter
            self.core_out[part(i)] = grads[rows_at(start, quarter)].astype(BF16)
            self.send(core_slots[i], self.core_out.at[part(i)], self.core_in.at[part(i)],
                      at.across())
        yield
        x_slots = self.slots(nx - 1)
        for i in range(nx):
            self.arrive(core_slots[i], self.core_in.at[part(i)], at.across())
            start = core * half + (x + 1 + i) % nx * quarter
            pair = grads[rows_at(start, quarter)] + self.core_in[part(i)].astype(F32)
            if i < nx - 1:
                self.x_out[i] = pair.astype(BF16)
                self.send(x_slots[i], self.x_out.at[i], self.x_in.at[i], at.along_x(i + 1))
            else:
                self.mine[...] = pair
        yield
        for i in range(nx - 1):
            self.arrive(x_slots[i], self.x_in.at[i], at.along_x(-i - 1))
            self.mine[...] += self.x_in[i].astype(F32)
        self.y_out[...] = self.mine[...].astype(BF16)
        y_slots = self.slots(NY - 1)
        for k in range(1, NY):
            self.send(y_slots[k - 1], self.y_out.at[rows_at((y + k) % NY * piece, piece)],
                      self.y_in.at[k - 1], at.along_y(k))
        yield
        summed = self.mine[rows_at(y * piece, piece)]
        for k in range(1, NY):
            self.arrive(y_slots[k - 1], self.y_in.at[k - 1], at.along_y(-k))
            summed = summed + self.y_in[k - 1].astype(F32)
        self.z_all[z] = summed.astype(BF16)
        z_slots = self.slots(nz - 1)
        for k in range(1, nz):
            self.send(z_slots[k - 1], self.z_all.at[z], self.z_all.at[z], at.along_z(k))
        yield
        for k in range(1, nz):
            self.arrive(z_slots[k - 1], self.z_all.at[(z - k) % nz], at.along_z(-k))
        summed = self.z_all[0].astype(F32)
        for layer in range(1, nz):
            summed = summed + self.z_all[layer].astype(F32)
        base = core * half + x * quarter

        def piece_rows(k):
            return rows_at(base + (y + k) % NY * piece, piece)

        self.total[piece_rows(0)] = summed.astype(BF16)
        y_slots = self.slots(NY - 1)
        for k in range(1, NY):
            self.send(y_slots[k - 1], self.total.at[piece_rows(0)], self.total.at[piece_rows(0)],
                      at.along_y(k))
        yield
        for k in range(1, NY):
            self.arrive(y_slots[k - 1], self.total.at[piece_rows(-k)], at.along_y(-k))

        def quarter_of(which, k):
            return rows_at(which * half + (x + k) % nx * quarter, quarter)

        x_slots, core_slots = self.slots(nx - 1), self.slots(nx)
        own = self.total.at[quarter_of(core, 0)]
        for k in range(1, nx):
            self.send(x_slots[k - 1], own, own, at.along_x(k))
        self.send(core_slots[0], own, own, at.across())
        self.save(quarter_of(core, 0))
        yield
        for k in range(1, nx):
            other = self.total.at[quarter_of(core, -k)]
            self.arrive(x_slots[k - 1], other, at.along_x(-k))
            self.send(core_slots[k], other, other, at.across())
            self.save(quarter_of(core, -k))
        yield
        for k in range(nx):
            self.arrive(core_slots[k], self.total.at[quarter_of(1 - core, -k)], at.across())
            self.save(quarter_of(1 - core, -k))
        yield

    def finish(self):
        for copy in self.sent:
            copy.wait_send()
        for copy in self.saved:
            copy.wait()


def mul(a, b, dims=NN):
    return lax.dot_general(a, b, dims, preferred_element_type=F32)


def padding_matrix():
    out = np.zeros((9, 2, 8, 8, 2, 128), np.float32)
    sides = ([(7, 0)], [(i, i + 1) for i in range(8)], [(0, 9)])
    for layer_y in range(3):
        for layer_z in range(3):
            for y, to_y in sides[layer_y]:
                for z, to_z in sides[layer_z]:
                    for half in range(2):
                        out[3 * layer_y + layer_z, half, y, z, half, 10 * to_y + to_z] = 1
    return out.reshape(9 * 128, 256).astype(jnp.bfloat16)


def tap_matrix():
    out = np.zeros((2, 128, 9, 2, 8, 8), np.float32)
    for tap in range(9):
        for y in range(8):
            for z in range(8):
                for half in range(2):
                    out[half, 10 * (y + tap // 3) + z + tap % 3, tap, half, y, z] = 1
    return out.reshape(256, 9 * 128).astype(jnp.bfloat16)


def octant_matrix():
    out = np.zeros((8, 8, 8, 8, 64), np.float32)
    for x in range(8):
        for y in range(8):
            for z in range(8):
                octant = x % 2 * 4 + y % 2 * 2 + z % 2
                out[x, y, z, octant, x // 2 * 16 + y // 2 * 4 + z // 2] = 1
    return out.reshape(512, 512).astype(jnp.bfloat16)


def placing_matrix():
    out = np.zeros((8, 2, 64, 8, 8, 8), np.float32)
    for octant in range(8):
        for v in range(64):
            x, y, z = v // 16, v // 4 % 4, v % 4
            spot = (octant // 4 * 4 + x, octant // 2 % 2 * 4 + y, octant % 2 * 4 + z)
            out[(octant, slice(None), v) + spot] = 1
    return out.reshape(1024, 512).astype(jnp.bfloat16)


def low_lanes(shape):
    return lax.broadcasted_iota(jnp.int32, shape, len(shape) - 1) % 128 < 64


def packed(block):
    return jnp.where(low_lanes((64, 128)), block[:64], block[64:])


def chosen(labels, slot, table):
    hit = jnp.where(labels[0:1] == slot, 1.0, 0.0).astype(BF16)
    return hit * table


def kernel(sizes, neighbours, owners, octslots, features, occupancy, *refs):
    held, (out_first, out_last, out_coarse) = refs[:7], refs[7:10]
    loaded, refs = refs[10:17], refs[17:]
    cotangent, w_sub, w_down, pad_m, tap_m, oct_m, place_m = loaded
    (load_sem, source, upper, lower, gathered, edge, window, active, act_oct, w_cat, w_pair,
     oct_pack, oct_out, oct_in, lab_out, lab_in, table, rep_out, rep_in, returned, ret_half,
     back, shifted, place_in, coarse, pair_send, pair_recv) = refs[:27]
    sums = refs[27:]
    at = Place(sizes)
    first_sum = GradSum(at, FIRST_PIECE, sums[:len(sums) // 2], out_first)
    last_sum = GradSum(at, LAST_PIECE, sums[len(sums) // 2:], out_last)
    nspace = at.nz * NY
    me = at.z * NY + at.y
    rep = at.x * 2 + at.core
    above, below = ((me + 1) % nspace, rep), ((me + nspace - 1) % nspace, rep)
    partners = at.sum_partners() + [above, below]
    barrier = pltpu.get_barrier_semaphore()
    for partner in partners:
        pl.semaphore_signal(barrier, inc=1, device_id=partner, device_id_type=MESH)
    loads = [pltpu.make_async_copy(src, dst, load_sem.at[i])
             for i, (src, dst) in enumerate(zip(held, loaded))]
    for copy in loads:
        copy.start()

    def link(slot, src, dst, device):
        return pltpu.make_async_remote_copy(
            src_ref=src, dst_ref=dst, send_sem=pair_send.at[slot], recv_sem=pair_recv.at[slot],
            device_id=device, device_id_type=MESH)

    started = []

    def send(slot, src, dst, device):
        copy = link(slot, src, dst, device)
        copy.start()
        started.append(copy)

    occ = occupancy[...].astype(BF16)
    for j in range(BRICKS):
        source[j] = features[j] * occ[j:j + 1]
    source[BRICKS] = jnp.zeros((FINE, 512), BF16)
    upper[BRICKS] = jnp.zeros((FINE, 128), BF16)
    lower[BRICKS] = jnp.zeros((FINE, 128), BF16)
    owner_of = [owners[j] % NY for j in range(BRICKS)]

    def brick_for(member):
        found = BRICKS
        for j in range(BRICKS):
            found = jnp.where(owner_of[j] == member, j, found)
        return found

    for k in range(NY):
        member = (at.y + k) % NY
        label = -1
        for j in range(BRICKS):
            label = jnp.where(owner_of[j] == member, octslots[j], label)
        lab_out[k] = jnp.full((8, 128), label, jnp.int32)

    pl.semaphore_wait(barrier, len(partners))
    own, head, tail = pl.ds(0, BRICKS), pl.ds(0, 128), pl.ds(384, 128)
    send(0, source.at[own, :, tail], lower.at[own], above)
    send(1, source.at[own, :, head], upper.at[own], below)
    for k in range(1, NY):
        send(1 + k, lab_out.at[k], lab_in.at[k], at.along_y(k))
    lab_in[0] = lab_out[0]

    for copy in loads:
        copy.wait()
    spread = mul(cotangent[...].reshape(2 * COARSE, 512), place_m[...], NT)
    for s in range(2):
        for m in range(8):
            block = spread[s * COARSE:(s + 1) * COARSE, m * 128:(m + 1) * 128]
            table[8 * s + m] = packed(block).astype(BF16)
    for kx in range(3):
        w_cat[kx * FINE:(kx + 1) * FINE] = jnp.concatenate(
            [w_sub[TAPS * kx + t] for t in range(TAPS)], axis=1)
    for pair in range(4):
        for parity in range(2):
            w_pair[pair * FINE:(pair + 1) * FINE, parity * 128:(parity + 1) * 128] = (
                w_down[2 * pair + parity])

    for k in range(NY):
        if k:
            link(1 + k, lab_out.at[k], lab_in.at[k], at.along_y(-k)).wait_recv()
        labels = lab_in[k]
        answer = chosen(labels, 0, table[0])
        for slot in range(1, 16):
            answer = answer + chosen(labels, slot, table[slot])
        if k:
            rep_out[k] = answer
            send(8 + k, rep_out.at[k], rep_in.at[k], at.along_y(-k))
        else:
            rep_in[0] = answer

    for j in range(BRICKS):
        for n in range(9):
            which = jnp.clip(neighbours[j, 9 + n] - BRICKS, 0, BRICKS)
            for p in range(4):
                row = (j * 4 + p) * FINE
                gathered[row:row + FINE, n * 128:(n + 1) * 128] = (
                    source[which, :, p * 128:(p + 1) * 128])
    planes = mul(gathered[...], pad_m[...]).astype(BF16)
    planes = mul(planes, tap_m[...]).astype(BF16)
    for j in range(BRICKS):
        for p in range(4):
            row, column = (j * 4 + p) * FINE, j * PLANES + p * 128
            for t in range(TAPS):
                window[t * FINE:(t + 1) * FINE, column:column + 128] = (
                    planes[row:row + FINE, t * 128:(t + 1) * 128])

    link(0, source.at[own, :, tail], lower.at[own], below).wait_recv()
    link(1, source.at[own, :, head], upper.at[own], above).wait_recv()
    low = low_lanes((FINE, 128))
    for j in range(BRICKS):
        for n in range(9):
            which_low = jnp.clip(neighbours[j, n], 0, BRICKS)
            which_high = jnp.clip(neighbours[j, 18 + n] - 2 * BRICKS, 0, BRICKS)
            edge[j * FINE:(j + 1) * FINE, n * 128:(n + 1) * 128] = jnp.where(
                low, upper[which_high], lower[which_low])
    planes = mul(edge[...], pad_m[...]).astype(BF16)
    planes = mul(planes, tap_m[...]).astype(BF16)
    for j in range(BRICKS):
        column = j * PLANES + 512
        for t in range(TAPS):
            window[t * FINE:(t + 1) * FINE, column:column + 128] = (
                planes[j * FINE:(j + 1) * FINE, t * 128:(t + 1) * 128])

    def turned(rows):
        return [pltpu.roll(rows[:, i * 128:(i + 1) * 128], 64, 1) for i in range(rows.shape[1] // 128)]

    for two in range(BRICKS // 2):
        columns = slice(2 * two * PLANES, 2 * (two + 1) * PLANES)
        wide = mul(w_cat[...], window[:, columns])
        for j in (2 * two, 2 * two + 1):
            brick = wide[:, j % 2 * PLANES:(j % 2 + 1) * PLANES]
            behind, ahead = turned(brick[:FINE]), turned(brick[2 * FINE:])
            for i in range(4):
                lanes = slice(i * 128, (i + 1) * 128)
                total = brick[FINE:2 * FINE, lanes]
                total = total + jnp.where(low, ahead[i], ahead[i + 1])
                total = total + jnp.where(low, behind[i - 1], behind[i])
                pre_act = total * occupancy[j:j + 1, lanes].astype(F32)
                active[j * FINE:(j + 1) * FINE, lanes] = jnp.maximum(pre_act, 0.0).astype(BF16)

    octants = mul(active[...], oct_m[...]).astype(BF16)
    for j in range(BRICKS):
        for pair in range(4):
            act_oct[pair * FINE:(pair + 1) * FINE, j * 128:(j + 1) * 128] = (
                octants[j * FINE:(j + 1) * FINE, pair * 128:(pair + 1) * 128])
    summed = mul(w_pair[...], act_oct[...], TN)
    for j in range(BRICKS):
        even = summed[:COARSE, j * 128:(j + 1) * 128]
        odd = summed[COARSE:, j * 128:(j + 1) * 128]
        both = jnp.where(low_lanes((COARSE, 128)), even, odd)
        both = both + pltpu.roll(both, 64, 1)
        oct_pack[j] = packed(both).astype(BF16)
    oct_pack[BRICKS] = jnp.zeros((64, 128), BF16)
    for k in range(NY):
        block = oct_pack[brick_for((at.y + k) % NY)]
        if k:
            oct_out[k] = block
            send(15 + k, oct_out.at[k], oct_in.at[k], at.along_y(k))
        else:
            oct_in[0] = block

    for k in range(1, NY):
        link(8 + k, rep_out.at[k], rep_in.at[k], at.along_y(k)).wait_recv()
    low_rows = low_lanes((64, 128))
    for j in range(BRICKS):
        block = rep_in[(owner_of[j] - at.y + NY) % NY].astype(F32)
        other = pltpu.roll(block, 64, 1)
        returned[0:64, j * 128:(j + 1) * 128] = jnp.where(low_rows, block, other).astype(BF16)
        returned[64:128, j * 128:(j + 1) * 128] = jnp.where(low_rows, other, block).astype(BF16)
    whole = returned[...].astype(F32)
    low_half = low_lanes((COARSE, 512))
    ret_half[:COARSE] = jnp.where(low_half, whole, 0.0).astype(BF16)
    ret_half[COARSE:] = jnp.where(low_half, 0.0, whole).astype(BF16)
    spread = mul(w_down[...].reshape(8 * FINE, COARSE), returned[...])
    low_half = low_lanes((FINE, 512))
    for pair in range(4):
        even = spread[2 * pair * FINE:(2 * pair + 1) * FINE]
        odd = spread[(2 * pair + 1) * FINE:(2 * pair + 2) * FINE]
        both = jnp.where(low_half, even, odd).astype(BF16)
        for j in range(BRICKS):
            back[j * FINE:(j + 1) * FINE, pair * 128:(pair + 1) * 128] = both[:, j * 128:(j + 1) * 128]
    grad_act = mul(back[...], oct_m[...], NT)
    grad_pre = jnp.where(active[...].astype(F32) > 0, grad_act, 0.0)
    for j in range(BRICKS):
        brick = grad_pre[j * FINE:(j + 1) * FINE]
        sides = turned(brick) + [jnp.zeros((FINE, 128), F32)]
        for i in range(5):
            lanes = slice(j * PLANES + i * 128, j * PLANES + (i + 1) * 128)
            middle = brick[:, i * 128:(i + 1) * 128] if i < 4 else sides[4]
            shifted[0:FINE, lanes] = jnp.where(low, sides[i], sides[(i + 1) % 5]).astype(BF16)
            shifted[FINE:2 * FINE, lanes] = middle.astype(BF16)
            shifted[2 * FINE:, lanes] = jnp.where(low, sides[i - 1], sides[i]).astype(BF16)

    split = FIRST_BLOCKS * 128
    part = mul(shifted[...], window[0:split], NT)
    for b in range(FIRST_BLOCKS):
        first_sum.grads[b * SUB_ROWS:(b + 1) * SUB_ROWS] = part[:, b * 128:(b + 1) * 128]
    part = mul(act_oct[...], ret_half[...], NT)
    for parity in range(2):
        start = DOWN_START + parity * DOWN_ROWS
        first_sum.grads[start:start + DOWN_ROWS] = part[:, parity * 128:(parity + 1) * 128]
    used = DOWN_START + 2 * DOWN_ROWS
    first_sum.grads[used:] = jnp.zeros((first_sum.grads.shape[0] - used, 128), F32)
    first = first_sum.phases()
    next(first)
    last_sum.grads[...] = jnp.zeros(last_sum.grads.shape, F32)
    part = mul(shifted[...], window[split:], NT)
    for b in range(LAST_BLOCKS):
        width = min(128, TAPS * FINE - split - b * 128)
        last_sum.grads[b * SUB_ROWS:(b + 1) * SUB_ROWS, 0:width] = part[:, b * 128:b * 128 + width]
    last = last_sum.phases()
    next(last)

    def place_octants():
        for k in range(1, NY):
            link(15 + k, oct_out.at[k], oct_in.at[k], at.along_y(-k)).wait_recv()
        for slot in range(16):
            s, m = slot // 8, slot % 8
            block = chosen(lab_in[0], slot, oct_in[0])
            for k in range(1, NY):
                block = block + chosen(lab_in[k], slot, oct_in[k])
            block = block.astype(F32)
            lanes = slice(m * 128, (m + 1) * 128)
            place_in[s * 128:s * 128 + 64, lanes] = jnp.where(low_rows, block, 0.0).astype(BF16)
            place_in[s * 128 + 64:s * 128 + 128, lanes] = jnp.where(low_rows, 0.0, block).astype(BF16)
        result = mul(place_in[...], place_m[...]).astype(BF16)
        for s in range(2):
            coarse[s] = result[s * COARSE:(s + 1) * COARSE]

    save = pltpu.make_async_copy(coarse, out_coarse, load_sem.at[len(loads)])
    for phase in range(1, 8):
        next(first)
        next(last)
        if phase == 2:
            place_octants()
            save.start()
    for copy in started:
        copy.wait_send()
    first_sum.finish()
    last_sum.finish()
    save.wait()


def unpack_kernel(first, last, coarse_in, coarse, grad_sub, grad_down, sub, down, sems):
    copies = [pltpu.make_async_copy(coarse_in, coarse, sems.at[0])]
    copies[0].start()
    for octant in range(8):
        row = DOWN_START + octant % 2 * DOWN_ROWS + octant // 2 * FINE
        down[octant] = first[row:row + FINE].astype(F32)
    copies.append(pltpu.make_async_copy(down, grad_down, sems.at[1]))
    copies[-1].start()

    def block(b, kx):
        ref, b = (first, b) if b < FIRST_BLOCKS else (last, b - FIRST_BLOCKS)
        row = b * SUB_ROWS + kx * FINE
        return ref[row:row + FINE].astype(F32)

    lane = lax.broadcasted_iota(jnp.int32, (FINE, 128), 1)
    for kx in range(3):
        for t in range(TAPS):
            b, offset = t * FINE // 128, t * FINE % 128
            left = block(b, kx)
            if offset:
                left = pltpu.roll(left, 128 - offset, 1)
            if offset > 32:
                right = pltpu.roll(block(b + 1, kx), 128 - offset, 1)
                left = jnp.where(lane < 128 - offset, left, right)
            sub[TAPS * kx + t] = left[:, :FINE]
        taps = pl.ds(TAPS * kx, TAPS)
        copies.append(pltpu.make_async_copy(sub.at[taps], grad_sub.at[taps], sems.at[2 + kx]))
        copies[-1].start()
    for copy in copies:
        copy.wait()


def per_device(sizes, features, occupancy, neighbours, owners, octslots, cotangent, w_sub, w_down):
    vmem = pl.BlockSpec(memory_space=pltpu.VMEM)
    smem = pl.BlockSpec(memory_space=pltpu.SMEM)
    hbm = pl.BlockSpec(memory_space=pl.ANY)
    v = pltpu.VMEM
    held = [cotangent[0], w_sub, jnp.transpose(w_down, (0, 2, 1)), jnp.asarray(padding_matrix()),
            jnp.asarray(tap_matrix()), jnp.asarray(octant_matrix()), jnp.asarray(placing_matrix())]
    rows = [sum_rows(sizes, piece) for piece in (FIRST_PIECE, LAST_PIECE)]
    first, last, coarse = pl.pallas_call(
        functools.partial(kernel, sizes),
        out_shape=(
            jax.ShapeDtypeStruct((rows[0], 128), BF16),
            jax.ShapeDtypeStruct((rows[1], 128), BF16),
            jax.ShapeDtypeStruct(cotangent.shape[1:], BF16),
        ),
        in_specs=[smem] * 3 + [vmem] * 2 + [hbm] * 7,
        out_specs=(hbm, hbm, hbm),
        scratch_shapes=[v(a.shape, a.dtype) for a in held] + [
            pltpu.SemaphoreType.DMA((8,)),
            v((BRICKS + 1, FINE, 512), BF16),
            v((BRICKS + 1, FINE, 128), BF16),
            v((BRICKS + 1, FINE, 128), BF16),
            v((BRICKS * 4 * FINE, TAPS * 128), BF16),
            v((BRICKS * FINE, TAPS * 128), BF16),
            v((TAPS * FINE, BRICKS * PLANES), BF16),
            v((BRICKS * FINE, 512), BF16),
            v((4 * FINE, BRICKS * 128), BF16),
            v((3 * FINE, TAPS * FINE), BF16),
            v((4 * FINE, 2 * COARSE), BF16),
            v((BRICKS + 1, 64, 128), BF16),
            v((NY, 64, 128), BF16),
            v((NY, 64, 128), BF16),
            v((NY, 8, 128), jnp.int32),
            v((NY, 8, 128), jnp.int32),
            v((16, 64, 128), BF16),
            v((NY, 64, 128), BF16),
            v((NY, 64, 128), BF16),
            v((COARSE, BRICKS * 128), BF16),
            v((2 * COARSE, BRICKS * 128), BF16),
            v((BRICKS * FINE, 512), BF16),
            v((3 * FINE, BRICKS * PLANES), BF16),
            v((2 * COARSE, 1024), BF16),
            v((2, COARSE, 512), BF16),
            pltpu.SemaphoreType.DMA((2 + 3 * (NY - 1),)),
            pltpu.SemaphoreType.DMA((2 + 3 * (NY - 1),)),
        ] + sum_scratch(sizes, FIRST_PIECE) + sum_scratch(sizes, LAST_PIECE),
        compiler_params=pltpu.CompilerParams(
            collective_id=0, has_side_effects=True, vmem_limit_bytes=56 * 2**20
        ),
    )(neighbours[0], owners[0], octslots[0], features[0], occupancy[0], *held)
    coarse, grad_sub, grad_down = pl.pallas_call(
        unpack_kernel,
        out_shape=(
            jax.ShapeDtypeStruct(cotangent.shape[1:], BF16),
            jax.ShapeDtypeStruct(w_sub.shape, F32),
            jax.ShapeDtypeStruct((8, FINE, COARSE), F32),
        ),
        in_specs=[vmem, vmem, hbm],
        out_specs=(hbm, hbm, hbm),
        scratch_shapes=[
            v(w_sub.shape, F32),
            v((8, FINE, COARSE), F32),
            pltpu.SemaphoreType.DMA((5,)),
        ],
        compiler_params=pltpu.CompilerParams(vmem_limit_bytes=32 * 2**20),
    )(first, last, coarse)
    return coarse[None], grad_sub, jnp.transpose(grad_down, (0, 2, 1))


def solution(mesh):
    sizes = (mesh.shape["space"] // NY, mesh.shape["rep"] // 2)
    return jax.shard_map(
        functools.partial(per_device, sizes),
        mesh=mesh,
        in_specs=(
            P("rep", "space", None, None),
            P("rep", "space", None),
            P("rep", "space", None),
            P("rep", "space"),
            P("rep", "space"),
            P("rep", "space", None, None),
            P(),
            P(),
        ),
        out_specs=(P("rep", "space", None, None), P(), P()),
        check_vma=False,
    )
```

time: 80.5 us -> 68.4 us (0.85)
  Pallas kernels: 73.1 us -> 64.6 us
  local copies, waits for them, and re-layouts: 6.59 us -> 2.93 us
    pallas_call x1, Pallas kernels: 73.1 us -> 63.3 us  [per_device(): pl.pallas_call(functools.partial(kernel, sizes), out_shape=(jax.ShapeDtyp...]
    unnamed x6, local copies, waits for them, and re-layouts: 6.59 us -> 2.93 us
    pallas_call x0 -> x1, Pallas kernels: none -> 1.32 us  [per_device(): pl.pallas_call(unpack_kernel, out_shape=(jax.ShapeDtypeStruct(cotangent.s...]
where the time goes in v1:
time: 68.4 us; the launch traced here: 68.2 us
  Pallas kernels  64.6 us (94%)
  local copies, waits for them, and re-layouts  2.93 us (4%)
    pallas_call x1, Pallas kernels, per_device(): pl.pallas_call(functools.partial(kernel, sizes), out_shape=(jax.ShapeDtyp...  63.3 us
    unnamed x6, local copies, waits for them, and re-layouts  2.93 us

profile of v1, /device:TPU:1, one launch (start us, length us, event | category | flops | bytes accessed | tf_op | source)
XLA Modules:
  0.0 68.2 jit_solution(9119154237941221787)
XLA Ops:
  0.6 63.3 %shard_map.139 = (bf16[2048,128]{1,0:T(8,128)(2,1)}, bf16[1024,128]{1,0:T(8,128)(2,1)}, bf16[2,128,512]{2,1,0:T(8,128)(2,1)}) custom-call(s32[4,27]{1,0:T(4,128)} %bitcast.13, s32[4]{0:T(128)} %bitcast.14, s32[4]{0:T(128)} %bitcast.15, bf16[4,96,512]{2,1,0:T(8,128)(2,1)} %bitcast.9, s32[4,512]{1,0:T(4,128)} %bitcast.12, bf16[2,128,512]{2,1,0:T(8,128)(2,1)} %bitcast.10, ...), custom_call_target="tpu_custom_call" | custom-call | tf_op jit(solution)/shard_map/pallas_call | solution.py:557
  63.9 0.0 copy-start
  63.9 1.0 %copy-done = bf16[2048,128]{1,0:T(8,128)(2,1)S(1)} copy-done((bf16[2048,128]{1,0:T(8,128)(2,1)S(1)}, bf16[2048,128]{1,0:T(8,128)(2,1)}, u32[]{:S(2)}) %copy-start) | copy-done | bytes 524312
  65.0 0.0 copy-start.1
  65.0 0.9 %copy-done.1 = bf16[1024,128]{1,0:T(8,128)(2,1)S(1)} copy-done((bf16[1024,128]{1,0:T(8,128)(2,1)S(1)}, bf16[1024,128]{1,0:T(8,128)(2,1)}, u32[]{:S(2)}) %copy-start.1) | copy-done | bytes 262168
  65.9 0.0 copy-start.2
  65.9 0.9 %copy-done.2 = bf16[2,128,512]{2,1,0:T(8,128)(2,1)S(1)} copy-done((bf16[2,128,512]{2,1,0:T(8,128)(2,1)S(1)}, bf16[2,128,512]{2,1,0:T(8,128)(2,1)}, u32[]{:S(2)}) %copy-start.2) | copy-done | bytes 262168
  66.9 1.3 %shard_map.140 = (bf16[2,128,512]{2,1,0:T(8,128)(2,1)}, f32[27,96,96]{2,1,0:T(8,128)}, f32[8,96,128]{2,1,0:T(8,128)}) custom-call(bf16[2048,128]{1,0:T(8,128)(2,1)S(1)} %copy-done, bf16[1024,128]{1,0:T(8,128)(2,1)S(1)} %copy-done.1, bf16[2,128,512]{2,1,0:T(8,128)(2,1)S(1)} %copy-done.2), custom_call_target="tpu_custom_call" | custom-call | tf_op jit(solution)/shard_map/pallas_call | solution.py:599
Async XLA Ops:
  63.9 1.0 %copy-start = (bf16[2048,128]{1,0:T(8,128)(2,1)S(1)}, bf16[2048,128]{1,0:T(8,128)(2,1)}, u32[]{:S(2)}) copy-start(bf16[2048,128]{1,0:T(8,128)(2,1)} %get-tuple-element.9.first) | copy-start | bytes 1572868
  65.0 0.9 %copy-start.1 = (bf16[1024,128]{1,0:T(8,128)(2,1)S(1)}, bf16[1024,128]{1,0:T(8,128)(2,1)}, u32[]{:S(2)}) copy-start(bf16[1024,128]{1,0:T(8,128)(2,1)} %get-tuple-element.10.last) | copy-start | bytes 786436
  65.9 0.9 %copy-start.2 = (bf16[2,128,512]{2,1,0:T(8,128)(2,1)S(1)}, bf16[2,128,512]{2,1,0:T(8,128)(2,1)}, u32[]{:S(2)}) copy-start(bf16[2,128,512]{2,1,0:T(8,128)(2,1)} %get-tuple-element.11.coarse_in) | copy-start | bytes 786436

commit v2 on v1

--- a/solution.py
+++ b/solution.py
@@ -21,11 +21,10 @@
 PLANES = 640
 SUB_ROWS = 3 * FINE
 DOWN_ROWS = 4 * FINE
-FIRST_BLOCKS = 4
-LAST_BLOCKS = 3
+SUB_BLOCKS = 7
 FIRST_PIECE = 32
 LAST_PIECE = 16
-DOWN_START = FIRST_BLOCKS * SUB_ROWS
+FIRST_ORDER, LAST_ORDER = "xyz", "yxz"
 
 
 class Place:
@@ -48,48 +47,59 @@
         return ((self.z + k) % self.nz * NY + self.y, self.x * 2 + self.core)
 
     def sum_partners(self):
-        near = [self.across()]
-        near += [self.along_x(k) for k in range(1, self.nx)]
-        near += [self.along_y(k) for k in range(1, NY)]
-        near += [self.along_z(k) for k in range(1, self.nz)]
-        return near
+        far = [self.along_y(k) for k in far_first(NY)]
+        far += [self.along_z(k) for k in far_first(self.nz)]
+        far += [self.along_x(k) for k in far_first(self.nx)]
+        return far + [self.across()]
 
 
 def rows_at(start, count):
     return pl.ds(pl.multiple_of(start, 16), count)
 
 
+def near_first(count):
+    return sorted(range(1, count), key=lambda k: min(k, count - k))
+
+
+def far_first(count):
+    return near_first(count)[::-1]
+
+
 def sum_rows(sizes, piece):
     return 2 * sizes[1] * NY * piece
 
 
-def sum_scratch(sizes, piece):
-    nz, nx = sizes
-    quarter = NY * piece
-    half = nx * quarter
-    copies = 2 * nx + 2 * (nx - 1) + 2 * (NY - 1) + (nz - 1)
+def axis_sizes(sizes, order):
+    return [{"x": sizes[1], "y": NY, "z": sizes[0]}[axis] for axis in order]
+
+
+def sum_scratch(sizes, piece, order):
+    na, nb, nc = axis_sizes(sizes, order)
+    share = nb * piece
+    half = na * share
+    copies = 2 * na + 2 * (na - 1) + 2 * (nb - 1) + (nc - 1)
     return [
         pltpu.VMEM((2 * half, 128), F32),
         pltpu.VMEM((half, 128), BF16),
         pltpu.VMEM((half, 128), BF16),
-        pltpu.VMEM((nx - 1, quarter, 128), BF16),
-        pltpu.VMEM((nx - 1, quarter, 128), BF16),
-        pltpu.VMEM((quarter, 128), F32),
-        pltpu.VMEM((quarter, 128), BF16),
-        pltpu.VMEM((NY - 1, piece, 128), BF16),
-        pltpu.VMEM((nz, piece, 128), BF16),
+        pltpu.VMEM((na - 1, share, 128), BF16),
+        pltpu.VMEM((na - 1, share, 128), BF16),
+        pltpu.VMEM((share, 128), F32),
+        pltpu.VMEM((share, 128), BF16),
+        pltpu.VMEM((nb - 1, piece, 128), BF16),
+        pltpu.VMEM((nc, piece, 128), BF16),
         pltpu.VMEM((2 * half, 128), BF16),
         pltpu.SemaphoreType.DMA((copies,)),
         pltpu.SemaphoreType.DMA((copies,)),
-        pltpu.SemaphoreType.DMA((2 * nx,)),
+        pltpu.SemaphoreType.DMA((2 * na,)),
     ]
 
 
 class GradSum:
-    def __init__(self, place, piece, scratch, result):
-        self.place, self.piece, self.result = place, piece, result
-        (self.grads, self.core_out, self.core_in, self.x_out, self.x_in, self.mine, self.y_out,
-         self.y_in, self.z_all, self.total, self.send_sem, self.recv_sem, self.save_sem) = scratch
+    def __init__(self, place, piece, order, scratch, result):
+        self.place, self.piece, self.order, self.result = place, piece, order, result
+        (self.grads, self.core_out, self.core_in, self.a_out, self.a_in, self.mine, self.b_out,
+         self.b_in, self.c_all, self.total, self.send_sem, self.recv_sem, self.save_sem) = scratch
         self.used = 0
         self.sent = []
         self.saved = []
@@ -111,102 +121,107 @@
             recv_sem=self.recv_sem.at[slot], device_id=device, device_id_type=MESH).wait_recv()
 
     def save(self, rows):
-        copy = pltpu.make_async_copy(
+        save = pltpu.make_async_copy(
             self.total.at[rows], self.result.at[rows], self.save_sem.at[len(self.saved)])
-        copy.start()
-        self.saved.append(copy)
+        save.start()
+        self.saved.append(save)
 
     def phases(self):
         at, piece, grads = self.place, self.piece, self.grads
-        nx, nz = at.nx, at.nz
-        quarter = NY * piece
-        half = nx * quarter
-        x, y, z, core = at.x, at.y, at.z, at.core
-
-        def part(i):
-            return rows_at((x + 1 + i) % nx * quarter, quarter)
-
-        core_slots = self.slots(nx)
-        for i in range(nx):
-            start = (1 - core) * half + (x + 1 + i) % nx * quarter
-            self.core_out[part(i)] = grads[rows_at(start, quarter)].astype(BF16)
-            self.send(core_slots[i], self.core_out.at[part(i)], self.core_in.at[part(i)],
+        na, nb, nc = axis_sizes((at.nz, at.nx), self.order)
+        a, b, c = [{"x": at.x, "y": at.y, "z": at.z}[axis] for axis in self.order]
+        along_a, along_b, along_c = [
+            {"x": at.along_x, "y": at.along_y, "z": at.along_z}[axis] for axis in self.order]
+        share = nb * piece
+        half = na * share
+        core = at.core
+
+        def part(k):
+            return rows_at((a + k) % na * share, share)
+
+        core_slots = self.slots(na)
+        for k in far_first(na) + [0]:
+            start = (1 - core) * half + (a + k) % na * share
+            self.core_out[part(k)] = grads[rows_at(start, share)].astype(BF16)
+            self.send(core_slots[k], self.core_out.at[part(k)], self.core_in.at[part(k)],
                       at.across())
         yield
-        x_slots = self.slots(nx - 1)
-        for i in range(nx):
-            self.arrive(core_slots[i], self.core_in.at[part(i)], at.across())
-            start = core * half + (x + 1 + i) % nx * quarter
-            pair = grads[rows_at(start, quarter)] + self.core_in[part(i)].astype(F32)
-            if i < nx - 1:
-                self.x_out[i] = pair.astype(BF16)
-                self.send(x_slots[i], self.x_out.at[i], self.x_in.at[i], at.along_x(i + 1))
+        a_slots = self.slots(na - 1)
+        for k in far_first(na) + [0]:
+            self.arrive(core_slots[k], self.core_in.at[part(k)], at.across())
+            start = core * half + (a + k) % na * share
+            pair = grads[rows_at(start, share)] + self.core_in[part(k)].astype(F32)
+            if k:
+                self.a_out[k - 1] = pair.astype(BF16)
+                self.send(a_slots[k - 1], self.a_out.at[k - 1], self.a_in.at[k - 1], along_a(k))
             else:
                 self.mine[...] = pair
         yield
-        for i in range(nx - 1):
-            self.arrive(x_slots[i], self.x_in.at[i], at.along_x(-i - 1))
-            self.mine[...] += self.x_in[i].astype(F32)
-        self.y_out[...] = self.mine[...].astype(BF16)
-        y_slots = self.slots(NY - 1)
-        for k in range(1, NY):
-            self.send(y_slots[k - 1], self.y_out.at[rows_at((y + k) % NY * piece, piece)],
-                      self.y_in.at[k - 1], at.along_y(k))
-        yield
-        summed = self.mine[rows_at(y * piece, piece)]
-        for k in range(1, NY):
-            self.arrive(y_slots[k - 1], self.y_in.at[k - 1], at.along_y(-k))
-            summed = summed + self.y_in[k - 1].astype(F32)
-        self.z_all[z] = summed.astype(BF16)
-        z_slots = self.slots(nz - 1)
-        for k in range(1, nz):
-            self.send(z_slots[k - 1], self.z_all.at[z], self.z_all.at[z], at.along_z(k))
-        yield
-        for k in range(1, nz):
-            self.arrive(z_slots[k - 1], self.z_all.at[(z - k) % nz], at.along_z(-k))
-        summed = self.z_all[0].astype(F32)
-        for layer in range(1, nz):
-            summed = summed + self.z_all[layer].astype(F32)
-        base = core * half + x * quarter
+        summed = self.mine[...]
+        for k in near_first(na):
+            self.arrive(a_slots[k - 1], self.a_in.at[k - 1], along_a(-k))
+            summed = summed + self.a_in[k - 1].astype(F32)
+        self.mine[...] = summed
+        self.b_out[...] = summed.astype(BF16)
+        b_slots = self.slots(nb - 1)
+        for k in far_first(nb):
+            self.send(b_slots[k - 1], self.b_out.at[rows_at((b + k) % nb * piece, piece)],
+                      self.b_in.at[k - 1], along_b(k))
+        yield
+        summed = self.mine[rows_at(b * piece, piece)]
+        for k in near_first(nb):
+            self.arrive(b_slots[k - 1], self.b_in.at[k - 1], along_b(-k))
+            summed = summed + self.b_in[k - 1].astype(F32)
+        self.c_all[c] = summed.astype(BF16)
+        c_slots = self.slots(nc - 1)
+        for k in far_first(nc):
+            self.send(c_slots[k - 1], self.c_all.at[c], self.c_all.at[c], along_c(k))
+        yield
+        for k in near_first(nc):
+            self.arrive(c_slots[k - 1], self.c_all.at[(c - k) % nc], along_c(-k))
+        summed = self.c_all[0].astype(F32)
+        for layer in range(1, nc):
+            summed = summed + self.c_all[layer].astype(F32)
+        base = core * half + a * share
 
         def piece_rows(k):
-            return rows_at(base + (y + k) % NY * piece, piece)
+            return rows_at(base + (b + k) % nb * piece, piece)
 
         self.total[piece_rows(0)] = summed.astype(BF16)
-        y_slots = self.slots(NY - 1)
-        for k in range(1, NY):
-            self.send(y_slots[k - 1], self.total.at[piece_rows(0)], self.total.at[piece_rows(0)],
-                      at.along_y(k))
-        yield
-        for k in range(1, NY):
-            self.arrive(y_slots[k - 1], self.total.at[piece_rows(-k)], at.along_y(-k))
-
-        def quarter_of(which, k):
-            return rows_at(which * half + (x + k) % nx * quarter, quarter)
-
-        x_slots, core_slots = self.slots(nx - 1), self.slots(nx)
-        own = self.total.at[quarter_of(core, 0)]
-        for k in range(1, nx):
-            self.send(x_slots[k - 1], own, own, at.along_x(k))
+        b_slots = self.slots(nb - 1)
+        for k in far_first(nb):
+            self.send(b_slots[k - 1], self.total.at[piece_rows(0)], self.total.at[piece_rows(0)],
+                      along_b(k))
+        yield
+        for k in near_first(nb):
+            self.arrive(b_slots[k - 1], self.total.at[piece_rows(-k)], along_b(-k))
+
+        def share_of(which, k):
+            return rows_at(which * half + (a + k) % na * share, share)
+
+        a_slots, core_slots = self.slots(na - 1), self.slots(na)
+        own = self.total.at[share_of(core, 0)]
+        for k in far_first(na):
+            self.send(a_slots[k - 1], own, own, along_a(k))
         self.send(core_slots[0], own, own, at.across())
-        self.save(quarter_of(core, 0))
-        yield
-        for k in range(1, nx):
-            other = self.total.at[quarter_of(core, -k)]
-            self.arrive(x_slots[k - 1], other, at.along_x(-k))
+        self.save(share_of(core, 0))
+        yield
+        for k in near_first(na):
+            other = self.total.at[share_of(core, -k)]
+            self.arrive(a_slots[k - 1], other, along_a(-k))
             self.send(core_slots[k], other, other, at.across())
-            self.save(quarter_of(core, -k))
-        yield
-        for k in range(nx):
-            self.arrive(core_slots[k], self.total.at[quarter_of(1 - core, -k)], at.across())
-            self.save(quarter_of(1 - core, -k))
+            self.save(share_of(core, -k))
+        yield
+        for k in [0] + near_first(na):
+            self.arrive(core_slots[k], self.total.at[share_of(1 - core, -k)], at.across())
+            self.save(share_of(1 - core, -k))
         yield
 
     def finish(self):
         for copy in self.sent:
             copy.wait_send()
-        for copy in self.saved:
-            copy.wait()
+        for save in self.saved:
+            save.wait()
 
 
 def mul(a, b, dims=NN):
@@ -268,17 +283,17 @@
     return hit * table
 
 
-def kernel(sizes, neighbours, owners, octslots, features, occupancy, *refs):
-    held, (out_first, out_last, out_coarse) = refs[:7], refs[7:10]
-    loaded, refs = refs[10:17], refs[17:]
-    cotangent, w_sub, w_down, pad_m, tap_m, oct_m, place_m = loaded
+def kernel(sizes, neighbours, owners, octslots, *refs):
+    held, (out_first, out_last, out_coarse) = refs[:9], refs[9:12]
+    loaded, refs = refs[12:21], refs[21:]
+    features, occupancy, pad_m, tap_m, cotangent, place_m, w_sub, w_down, oct_m = loaded
     (load_sem, source, upper, lower, gathered, edge, window, active, act_oct, w_cat, w_pair,
      oct_pack, oct_out, oct_in, lab_out, lab_in, table, rep_out, rep_in, returned, ret_half,
      back, shifted, place_in, coarse, pair_send, pair_recv) = refs[:27]
     sums = refs[27:]
     at = Place(sizes)
-    first_sum = GradSum(at, FIRST_PIECE, sums[:len(sums) // 2], out_first)
-    last_sum = GradSum(at, LAST_PIECE, sums[len(sums) // 2:], out_last)
+    first_sum = GradSum(at, FIRST_PIECE, FIRST_ORDER, sums[:len(sums) // 2], out_first)
+    last_sum = GradSum(at, LAST_PIECE, LAST_ORDER, sums[len(sums) // 2:], out_last)
     nspace = at.nz * NY
     me = at.z * NY + at.y
     rep = at.x * 2 + at.core
@@ -289,8 +304,8 @@
         pl.semaphore_signal(barrier, inc=1, device_id=partner, device_id_type=MESH)
     loads = [pltpu.make_async_copy(src, dst, load_sem.at[i])
              for i, (src, dst) in enumerate(zip(held, loaded))]
-    for copy in loads:
-        copy.start()
+    for load in loads:
+        load.start()
 
     def link(slot, src, dst, device):
         return pltpu.make_async_remote_copy(
@@ -304,6 +319,8 @@
         copy.start()
         started.append(copy)
 
+    for load in loads[:2]:
+        load.wait()
     occ = occupancy[...].astype(BF16)
     for j in range(BRICKS):
         source[j] = features[j] * occ[j:j + 1]
@@ -325,16 +342,42 @@
             label = jnp.where(owner_of[j] == member, octslots[j], label)
         lab_out[k] = jnp.full((8, 128), label, jnp.int32)
 
+    first_sum.grads[(SUB_BLOCKS - 1) * SUB_ROWS:] = jnp.zeros(
+        (first_sum.grads.shape[0] - (SUB_BLOCKS - 1) * SUB_ROWS, 128), F32)
+    last_sum.grads[2 * DOWN_ROWS:] = jnp.zeros((last_sum.grads.shape[0] - 2 * DOWN_ROWS, 128), F32)
+
+    def own_planes(bricks):
+        for j in bricks:
+            for n in range(9):
+                which = jnp.clip(neighbours[j, 9 + n] - BRICKS, 0, BRICKS)
+                for p in range(4):
+                    row = (j * 4 + p) * FINE
+                    gathered[row:row + FINE, n * 128:(n + 1) * 128] = (
+                        source[which, :, p * 128:(p + 1) * 128])
+        start = bricks[0] * 4 * FINE
+        planes = mul(gathered[start:start + len(bricks) * 4 * FINE], pad_m[...]).astype(BF16)
+        planes = mul(planes, tap_m[...]).astype(BF16)
+        for j in bricks:
+            for p in range(4):
+                row, column = (j * 4 + p) * FINE - start, j * PLANES + p * 128
+                for t in range(TAPS):
+                    window[t * FINE:(t + 1) * FINE, column:column + 128] = (
+                        planes[row:row + FINE, t * 128:(t + 1) * 128])
+
+    for load in loads[2:4]:
+        load.wait()
+    own_planes(range(2))
     pl.semaphore_wait(barrier, len(partners))
     own, head, tail = pl.ds(0, BRICKS), pl.ds(0, 128), pl.ds(384, 128)
+    for k in far_first(NY):
+        send(1 + k, lab_out.at[k], lab_in.at[k], at.along_y(k))
     send(0, source.at[own, :, tail], lower.at[own], above)
     send(1, source.at[own, :, head], upper.at[own], below)
-    for k in range(1, NY):
-        send(1 + k, lab_out.at[k], lab_in.at[k], at.along_y(k))
     lab_in[0] = lab_out[0]
 
-    for copy in loads:
-        copy.wait()
+    own_planes(range(2, BRICKS))
+    for load in loads[4:]:
+        load.wait()
     spread = mul(cotangent[...].reshape(2 * COARSE, 512), place_m[...], NT)
     for s in range(2):
         for m in range(8):
@@ -348,7 +391,7 @@
             w_pair[pair * FINE:(pair + 1) * FINE, parity * 128:(parity + 1) * 128] = (
                 w_down[2 * pair + parity])
 
-    for k in range(NY):
+    for k in [0] + near_first(NY):
         if k:
             link(1 + k, lab_out.at[k], lab_in.at[k], at.along_y(-k)).wait_recv()
         labels = lab_in[k]
@@ -360,22 +403,6 @@
             send(8 + k, rep_out.at[k], rep_in.at[k], at.along_y(-k))
         else:
             rep_in[0] = answer
-
-    for j in range(BRICKS):
-        for n in range(9):
-            which = jnp.clip(neighbours[j, 9 + n] - BRICKS, 0, BRICKS)
-            for p in range(4):
-                row = (j * 4 + p) * FINE
-                gathered[row:row + FINE, n * 128:(n + 1) * 128] = (
-                    source[which, :, p * 128:(p + 1) * 128])
-    planes = mul(gathered[...], pad_m[...]).astype(BF16)
-    planes = mul(planes, tap_m[...]).astype(BF16)
-    for j in range(BRICKS):
-        for p in range(4):
-            row, column = (j * 4 + p) * FINE, j * PLANES + p * 128
-            for t in range(TAPS):
-                window[t * FINE:(t + 1) * FINE, column:column + 128] = (
-                    planes[row:row + FINE, t * 128:(t + 1) * 128])
 
     link(0, source.at[own, :, tail], lower.at[own], below).wait_recv()
     link(1, source.at[own, :, head], upper.at[own], above).wait_recv()
@@ -424,7 +451,7 @@
         both = both + pltpu.roll(both, 64, 1)
         oct_pack[j] = packed(both).astype(BF16)
     oct_pack[BRICKS] = jnp.zeros((64, 128), BF16)
-    for k in range(NY):
+    for k in far_first(NY) + [0]:
         block = oct_pack[brick_for((at.y + k) % NY)]
         if k:
             oct_out[k] = block
@@ -464,23 +491,15 @@
             shifted[FINE:2 * FINE, lanes] = middle.astype(BF16)
             shifted[2 * FINE:, lanes] = jnp.where(low, sides[i - 1], sides[i]).astype(BF16)
 
-    split = FIRST_BLOCKS * 128
-    part = mul(shifted[...], window[0:split], NT)
-    for b in range(FIRST_BLOCKS):
-        first_sum.grads[b * SUB_ROWS:(b + 1) * SUB_ROWS] = part[:, b * 128:(b + 1) * 128]
+    part = mul(shifted[...], window[...], NT)
+    for b in range(SUB_BLOCKS):
+        width = min(128, TAPS * FINE - b * 128)
+        first_sum.grads[b * SUB_ROWS:(b + 1) * SUB_ROWS, 0:width] = part[:, b * 128:b * 128 + width]
+    first = first_sum.phases()
+    next(first)
     part = mul(act_oct[...], ret_half[...], NT)
     for parity in range(2):
-        start = DOWN_START + parity * DOWN_ROWS
-        first_sum.grads[start:start + DOWN_ROWS] = part[:, parity * 128:(parity + 1) * 128]
-    used = DOWN_START + 2 * DOWN_ROWS
-    first_sum.grads[used:] = jnp.zeros((first_sum.grads.shape[0] - used, 128), F32)
-    first = first_sum.phases()
-    next(first)
-    last_sum.grads[...] = jnp.zeros(last_sum.grads.shape, F32)
-    part = mul(shifted[...], window[split:], NT)
-    for b in range(LAST_BLOCKS):
-        width = min(128, TAPS * FINE - split - b * 128)
-        last_sum.grads[b * SUB_ROWS:(b + 1) * SUB_ROWS, 0:width] = part[:, b * 128:b * 128 + width]
+        last_sum.grads[parity * DOWN_ROWS:(parity + 1) * DOWN_ROWS] = part[:, parity * 128:(parity + 1) * 128]
     last = last_sum.phases()
     next(last)
 
@@ -501,12 +520,12 @@
             coarse[s] = result[s * COARSE:(s + 1) * COARSE]
 
     save = pltpu.make_async_copy(coarse, out_coarse, load_sem.at[len(loads)])
-    for phase in range(1, 8):
-        next(first)
-        next(last)
-        if phase == 2:
-            place_octants()
-            save.start()
+    for chunk in (first, last, first, last):
+        next(chunk)
+    place_octants()
+    save.start()
+    for chunk in (first, last, first, last, last, first, first, last, first, last):
+        next(chunk)
     for copy in started:
         copy.wait_send()
     first_sum.finish()
@@ -518,15 +537,14 @@
     copies = [pltpu.make_async_copy(coarse_in, coarse, sems.at[0])]
     copies[0].start()
     for octant in range(8):
-        row = DOWN_START + octant % 2 * DOWN_ROWS + octant // 2 * FINE
-        down[octant] = first[row:row + FINE].astype(F32)
+        row = octant % 2 * DOWN_ROWS + octant // 2 * FINE
+        down[octant] = last[row:row + FINE].astype(F32)
     copies.append(pltpu.make_async_copy(down, grad_down, sems.at[1]))
     copies[-1].start()
 
     def block(b, kx):
-        ref, b = (first, b) if b < FIRST_BLOCKS else (last, b - FIRST_BLOCKS)
         row = b * SUB_ROWS + kx * FINE
-        return ref[row:row + FINE].astype(F32)
+        return first[row:row + FINE].astype(F32)
 
     lane = lax.broadcasted_iota(jnp.int32, (FINE, 128), 1)
     for kx in range(3):
@@ -551,8 +569,9 @@
     smem = pl.BlockSpec(memory_space=pltpu.SMEM)
     hbm = pl.BlockSpec(memory_space=pl.ANY)
     v = pltpu.VMEM
-    held = [cotangent[0], w_sub, jnp.transpose(w_down, (0, 2, 1)), jnp.asarray(padding_matrix()),
-            jnp.asarray(tap_matrix()), jnp.asarray(octant_matrix()), jnp.asarray(placing_matrix())]
+    held = [features[0], occupancy[0], jnp.asarray(padding_matrix()), jnp.asarray(tap_matrix()),
+            cotangent[0], jnp.asarray(placing_matrix()), w_sub, jnp.transpose(w_down, (0, 2, 1)),
+            jnp.asarray(octant_matrix())]
     rows = [sum_rows(sizes, piece) for piece in (FIRST_PIECE, LAST_PIECE)]
     first, last, coarse = pl.pallas_call(
         functools.partial(kernel, sizes),
@@ -561,10 +580,10 @@
             jax.ShapeDtypeStruct((rows[1], 128), BF16),
             jax.ShapeDtypeStruct(cotangent.shape[1:], BF16),
         ),
-        in_specs=[smem] * 3 + [vmem] * 2 + [hbm] * 7,
+        in_specs=[smem] * 3 + [hbm] * 9,
         out_specs=(hbm, hbm, hbm),
         scratch_shapes=[v(a.shape, a.dtype) for a in held] + [
-            pltpu.SemaphoreType.DMA((8,)),
+            pltpu.SemaphoreType.DMA((10,)),
             v((BRICKS + 1, FINE, 512), BF16),
             v((BRICKS + 1, FINE, 128), BF16),
             v((BRICKS + 1, FINE, 128), BF16),
@@ -591,11 +610,11 @@
             v((2, COARSE, 512), BF16),
             pltpu.SemaphoreType.DMA((2 + 3 * (NY - 1),)),
             pltpu.SemaphoreType.DMA((2 + 3 * (NY - 1),)),
-        ] + sum_scratch(sizes, FIRST_PIECE) + sum_scratch(sizes, LAST_PIECE),
+        ] + sum_scratch(sizes, FIRST_PIECE, FIRST_ORDER) + sum_scratch(sizes, LAST_PIECE, LAST_ORDER),
         compiler_params=pltpu.CompilerParams(
             collective_id=0, has_side_effects=True, vmem_limit_bytes=56 * 2**20
         ),
-    )(neighbours[0], owners[0], octslots[0], features[0], occupancy[0], *held)
+    )(neighbours[0], owners[0], octslots[0], *held)
     coarse, grad_sub, grad_down = pl.pallas_call(
         unpack_kernel,
         out_shape=(
@@ -603,14 +622,14 @@
             jax.ShapeDtypeStruct(w_sub.shape, F32),
             jax.ShapeDtypeStruct((8, FINE, COARSE), F32),
         ),
-        in_specs=[vmem, vmem, hbm],
+        in_specs=[vmem, vmem, vmem],
         out_specs=(hbm, hbm, hbm),
         scratch_shapes=[
             v(w_sub.shape, F32),
             v((8, FINE, COARSE), F32),
             pltpu.SemaphoreType.DMA((5,)),
         ],
-        compiler_params=pltpu.CompilerParams(vmem_limit_bytes=32 * 2**20),
+        compiler_params=pltpu.CompilerParams(vmem_limit_bytes=56 * 2**20),
     )(first, last, coarse)
     return coarse[None], grad_sub, jnp.transpose(grad_down, (0, 2, 1))
 

time: 68.4 us -> 59.9 us (0.88)
  Pallas kernels: 64.6 us -> 59.1 us
  local copies, waits for them, and re-layouts: 2.93 us -> 0 us
    pallas_call x1, Pallas kernels: 63.3 us -> 56.6 us  [per_device(): pl.pallas_call(functools.partial(kernel, sizes), out_shape=(jax.ShapeDtyp...]
    unnamed x6 -> x0, local copies, waits for them, and re-layouts: 2.93 us -> none
    pallas_call x1, Pallas kernels: 1.32 us -> 2.51 us  [per_device(): pl.pallas_call(unpack_kernel, out_shape=(jax.ShapeDtypeStruct(cotangent.s...]
where the time goes in v2:
time: 59.9 us; the launch traced here: 59.7 us
  Pallas kernels  59.1 us (99%)
  between operations  0.64 us (1%)
    pallas_call x1, Pallas kernels, per_device(): pl.pallas_call(functools.partial(kernel, sizes), out_shape=(jax.ShapeDtyp...  56.6 us
    pallas_call x1, Pallas kernels, per_device(): pl.pallas_call(unpack_kernel, out_shape=(jax.ShapeDtypeStruct(cotangent.s...  2.51 us

profile of v2, /device:TPU:1, one launch (start us, length us, event | category | flops | bytes accessed | tf_op | source)
XLA Modules:
  0.0 59.7 jit_solution(3211739245940417717)
XLA Ops:
  0.6 56.6 %shard_map.139 = (bf16[2048,128]{1,0:T(8,128)(2,1)}, bf16[1024,128]{1,0:T(8,128)(2,1)}, bf16[2,128,512]{2,1,0:T(8,128)(2,1)}) custom-call(s32[4,27]{1,0:T(4,128)} %bitcast.13, s32[4]{0:T(128)} %bitcast.14, s32[4]{0:T(128)} %bitcast.15, bf16[4,96,512]{2,1,0:T(8,128)(2,1)} %bitcast.9, s32[4,512]{1,0:T(4,128)} %bitcast.12, ...), custom_call_target="tpu_custom_call" | custom-call | tf_op jit(solution)/shard_map/pallas_call | solution.py:576
  57.2 2.5 %shard_map.140 = (bf16[2,128,512]{2,1,0:T(8,128)(2,1)}, f32[27,96,96]{2,1,0:T(8,128)}, f32[8,96,128]{2,1,0:T(8,128)}) custom-call(bf16[2048,128]{1,0:T(8,128)(2,1)} %get-tuple-element.9.first, bf16[1024,128]{1,0:T(8,128)(2,1)} %get-tuple-element.10.last, bf16[2,128,512]{2,1,0:T(8,128)(2,1)} %get-tuple-element.11.coarse_in), custom_call_target="tpu_custom_call" | custom-call | tf_op jit(solution)/shard_map/pallas_call | solution.py:618

commit v3 on v2

--- a/solution.py
+++ b/solution.py
@@ -22,9 +22,10 @@
 SUB_ROWS = 3 * FINE
 DOWN_ROWS = 4 * FINE
 SUB_BLOCKS = 7
-FIRST_PIECE = 32
-LAST_PIECE = 16
-FIRST_ORDER, LAST_ORDER = "xyz", "yxz"
+PIECE = 48
+SHARE = NY * PIECE
+DOWN_START = SUB_BLOCKS * SUB_ROWS
+USED_ROWS = DOWN_START + 2 * DOWN_ROWS
 
 
 class Place:
@@ -37,19 +38,26 @@
     def across(self):
         return (self.z * NY + self.y, self.x * 2 + 1 - self.core)
 
-    def along_x(self, k):
-        return (self.z * NY + self.y, (self.x + k) % self.nx * 2 + self.core)
-
     def along_y(self, k):
         return (self.z * NY + (self.y + k) % NY, self.x * 2 + self.core)
 
     def along_z(self, k):
         return ((self.z + k) % self.nz * NY + self.y, self.x * 2 + self.core)
 
+    def in_plane(self, i, k):
+        y = (self.y + k * (1 - self.core)) % NY
+        z = (self.z + k * self.core) % NY
+        return (z * NY + y, (self.x + i) % self.nx * 2 + self.core)
+
+    def across_planes(self, k):
+        y = (self.y + k * self.core) % NY
+        z = (self.z + k * (1 - self.core)) % NY
+        return (z * NY + y, self.x * 2 + self.core)
+
     def sum_partners(self):
         far = [self.along_y(k) for k in far_first(NY)]
-        far += [self.along_z(k) for k in far_first(self.nz)]
-        far += [self.along_x(k) for k in far_first(self.nx)]
+        far += [self.in_plane(i, k) for i in far_first(self.nx) for k in far_first(NY) + [0]]
+        far += [self.along_z(k) for k in far_first(NY)]
         return far + [self.across()]
 
 
@@ -65,41 +73,29 @@
     return near_first(count)[::-1]
 
 
-def sum_rows(sizes, piece):
-    return 2 * sizes[1] * NY * piece
-
-
-def axis_sizes(sizes, order):
-    return [{"x": sizes[1], "y": NY, "z": sizes[0]}[axis] for axis in order]
-
-
-def sum_scratch(sizes, piece, order):
-    na, nb, nc = axis_sizes(sizes, order)
-    share = nb * piece
-    half = na * share
-    copies = 2 * na + 2 * (na - 1) + 2 * (nb - 1) + (nc - 1)
+def sum_scratch(nx):
+    half = nx * SHARE
+    copies = 2 * nx + 2 * nx * NY + NY
     return [
         pltpu.VMEM((2 * half, 128), F32),
         pltpu.VMEM((half, 128), BF16),
         pltpu.VMEM((half, 128), BF16),
-        pltpu.VMEM((na - 1, share, 128), BF16),
-        pltpu.VMEM((na - 1, share, 128), BF16),
-        pltpu.VMEM((share, 128), F32),
-        pltpu.VMEM((share, 128), BF16),
-        pltpu.VMEM((nb - 1, piece, 128), BF16),
-        pltpu.VMEM((nc, piece, 128), BF16),
+        pltpu.VMEM((nx, SHARE, 128), BF16),
+        pltpu.VMEM((nx * NY, PIECE, 128), BF16),
+        pltpu.VMEM((SHARE, 128), F32),
+        pltpu.VMEM((NY, PIECE, 128), BF16),
         pltpu.VMEM((2 * half, 128), BF16),
         pltpu.SemaphoreType.DMA((copies,)),
         pltpu.SemaphoreType.DMA((copies,)),
-        pltpu.SemaphoreType.DMA((2 * na,)),
+        pltpu.SemaphoreType.DMA((2 * nx,)),
     ]
 
 
 class GradSum:
-    def __init__(self, place, piece, order, scratch, result):
-        self.place, self.piece, self.order, self.result = place, piece, order, result
-        (self.grads, self.core_out, self.core_in, self.a_out, self.a_in, self.mine, self.b_out,
-         self.b_in, self.c_all, self.total, self.send_sem, self.recv_sem, self.save_sem) = scratch
+    def __init__(self, place, scratch, result):
+        self.place, self.result = place, result
+        (self.grads, self.core_out, self.core_in, self.plane_out, self.plane_in, self.mine,
+         self.across_all, self.total, self.send_sem, self.recv_sem, self.save_sem) = scratch
         self.used = 0
         self.sent = []
         self.saved = []
@@ -126,96 +122,84 @@
         save.start()
         self.saved.append(save)
 
-    def phases(self):
-        at, piece, grads = self.place, self.piece, self.grads
-        na, nb, nc = axis_sizes((at.nz, at.nx), self.order)
-        a, b, c = [{"x": at.x, "y": at.y, "z": at.z}[axis] for axis in self.order]
-        along_a, along_b, along_c = [
-            {"x": at.along_x, "y": at.along_y, "z": at.along_z}[axis] for axis in self.order]
-        share = nb * piece
-        half = na * share
+    def start(self):
+        at, grads = self.place, self.grads
+        half = at.nx * SHARE
+        self.core_slots = self.slots(at.nx)
+        self.far_x = far_first(at.nx) + [0]
+        self.near_x = self.far_x[::-1]
+        for i in self.far_x:
+            rows = self.share(i)
+            start = (1 - at.core) * half + (at.x + i) % at.nx * SHARE
+            self.core_out[rows] = grads[rows_at(start, SHARE)].astype(BF16)
+            self.send(self.core_slots[i], self.core_out.at[rows], self.core_in.at[rows], at.across())
+
+    def share(self, i):
+        return rows_at((self.place.x + i) % self.place.nx * SHARE, SHARE)
+
+    def run(self, meanwhile):
+        at, grads, nx = self.place, self.grads, self.place.nx
+        half = nx * SHARE
         core = at.core
-
-        def part(k):
-            return rows_at((a + k) % na * share, share)
-
-        core_slots = self.slots(na)
-        for k in far_first(na) + [0]:
-            start = (1 - core) * half + (a + k) % na * share
-            self.core_out[part(k)] = grads[rows_at(start, share)].astype(BF16)
-            self.send(core_slots[k], self.core_out.at[part(k)], self.core_in.at[part(k)],
-                      at.across())
-        yield
-        a_slots = self.slots(na - 1)
-        for k in far_first(na) + [0]:
-            self.arrive(core_slots[k], self.core_in.at[part(k)], at.across())
-            start = core * half + (a + k) % na * share
-            pair = grads[rows_at(start, share)] + self.core_in[part(k)].astype(F32)
-            if k:
-                self.a_out[k - 1] = pair.astype(BF16)
-                self.send(a_slots[k - 1], self.a_out.at[k - 1], self.a_in.at[k - 1], along_a(k))
-            else:
+        b = core * at.z + (1 - core) * at.y
+        c = core * at.y + (1 - core) * at.z
+        far, near = far_first(NY) + [0], [0] + near_first(NY)
+        slots = self.slots(nx * NY)
+        for i in self.far_x:
+            rows = self.share(i)
+            self.arrive(self.core_slots[i], self.core_in.at[rows], at.across())
+            start = core * half + (at.x + i) % nx * SHARE
+            pair = grads[rows_at(start, SHARE)] + self.core_in[rows].astype(F32)
+            self.plane_out[i] = pair.astype(BF16)
+            if i == 0:
                 self.mine[...] = pair
-        yield
-        summed = self.mine[...]
-        for k in near_first(na):
-            self.arrive(a_slots[k - 1], self.a_in.at[k - 1], along_a(-k))
-            summed = summed + self.a_in[k - 1].astype(F32)
-        self.mine[...] = summed
-        self.b_out[...] = summed.astype(BF16)
-        b_slots = self.slots(nb - 1)
-        for k in far_first(nb):
-            self.send(b_slots[k - 1], self.b_out.at[rows_at((b + k) % nb * piece, piece)],
-                      self.b_in.at[k - 1], along_b(k))
-        yield
-        summed = self.mine[rows_at(b * piece, piece)]
-        for k in near_first(nb):
-            self.arrive(b_slots[k - 1], self.b_in.at[k - 1], along_b(-k))
-            summed = summed + self.b_in[k - 1].astype(F32)
-        self.c_all[c] = summed.astype(BF16)
-        c_slots = self.slots(nc - 1)
-        for k in far_first(nc):
-            self.send(c_slots[k - 1], self.c_all.at[c], self.c_all.at[c], along_c(k))
-        yield
-        for k in near_first(nc):
-            self.arrive(c_slots[k - 1], self.c_all.at[(c - k) % nc], along_c(-k))
-        summed = self.c_all[0].astype(F32)
-        for layer in range(1, nc):
-            summed = summed + self.c_all[layer].astype(F32)
-        base = core * half + a * share
-
-        def piece_rows(k):
-            return rows_at(base + (b + k) % nb * piece, piece)
-
-        self.total[piece_rows(0)] = summed.astype(BF16)
-        b_slots = self.slots(nb - 1)
-        for k in far_first(nb):
-            self.send(b_slots[k - 1], self.total.at[piece_rows(0)], self.total.at[piece_rows(0)],
-                      along_b(k))
-        yield
-        for k in near_first(nb):
-            self.arrive(b_slots[k - 1], self.total.at[piece_rows(-k)], along_b(-k))
-
-        def share_of(which, k):
-            return rows_at(which * half + (a + k) % na * share, share)
-
-        a_slots, core_slots = self.slots(na - 1), self.slots(na)
-        own = self.total.at[share_of(core, 0)]
-        for k in far_first(na):
-            self.send(a_slots[k - 1], own, own, along_a(k))
-        self.send(core_slots[0], own, own, at.across())
-        self.save(share_of(core, 0))
-        yield
-        for k in near_first(na):
-            other = self.total.at[share_of(core, -k)]
-            self.arrive(a_slots[k - 1], other, along_a(-k))
-            self.send(core_slots[k], other, other, at.across())
-            self.save(share_of(core, -k))
-        yield
-        for k in [0] + near_first(na):
-            self.arrive(core_slots[k], self.total.at[share_of(1 - core, -k)], at.across())
-            self.save(share_of(1 - core, -k))
-        yield
+            for k in far:
+                if i or k:
+                    self.send(slots[i * NY + k],
+                              self.plane_out.at[i, rows_at((b + k) % NY * PIECE, PIECE)],
+                              self.plane_in.at[i * NY + k], at.in_plane(i, k))
+        meanwhile()
+        summed = self.mine[rows_at(b * PIECE, PIECE)]
+        for i in self.near_x:
+            for k in near:
+                if i or k:
+                    slot = i * NY + k
+                    self.arrive(slots[slot], self.plane_in.at[slot], at.in_plane(-i, -k))
+                    summed = summed + self.plane_in[slot].astype(F32)
+        self.across_all[c] = summed.astype(BF16)
+        slots = self.slots(NY)
+        for k in far_first(NY):
+            self.send(slots[k], self.across_all.at[c], self.across_all.at[c], at.across_planes(k))
+        for k in near_first(NY):
+            self.arrive(slots[k], self.across_all.at[(c - k) % NY], at.across_planes(-k))
+        summed = self.across_all[0].astype(F32)
+        for layer in range(1, NY):
+            summed = summed + self.across_all[layer].astype(F32)
+
+        def share_of(which, i):
+            return rows_at(which * half + (at.x + i) % nx * SHARE, SHARE)
+
+        def piece_of(i, k):
+            start = core * half + (at.x + i) % nx * SHARE + (b + k) % NY * PIECE
+            return self.total.at[rows_at(start, PIECE)]
+
+        self.total[rows_at(core * half + at.x * SHARE + b * PIECE, PIECE)] = summed.astype(BF16)
+        slots = self.slots(nx * NY)
+        for i in self.far_x:
+            for k in far:
+                if i or k:
+                    self.send(slots[i * NY + k], piece_of(0, 0), piece_of(0, 0), at.in_plane(i, k))
+        core_slots = self.slots(nx)
+        for i in self.near_x:
+            for k in near:
+                if i or k:
+                    self.arrive(slots[i * NY + k], piece_of(-i, -k), at.in_plane(-i, -k))
+            other = self.total.at[share_of(core, -i)]
+            self.send(core_slots[i], other, other, at.across())
+            self.save(share_of(core, -i))
+        for i in self.near_x:
+            self.arrive(core_slots[i], self.total.at[share_of(1 - core, -i)], at.across())
+            self.save(share_of(1 - core, -i))
 
     def finish(self):
         for copy in self.sent:
@@ -284,16 +268,15 @@
 
 
 def kernel(sizes, neighbours, owners, octslots, *refs):
-    held, (out_first, out_last, out_coarse) = refs[:9], refs[9:12]
-    loaded, refs = refs[12:21], refs[21:]
+    held, (out_total, out_coarse) = refs[:9], refs[9:11]
+    loaded, refs = refs[11:20], refs[20:]
     features, occupancy, pad_m, tap_m, cotangent, place_m, w_sub, w_down, oct_m = loaded
     (load_sem, source, upper, lower, gathered, edge, window, active, act_oct, w_cat, w_pair,
      oct_pack, oct_out, oct_in, lab_out, lab_in, table, rep_out, rep_in, returned, ret_half,
      back, shifted, place_in, coarse, pair_send, pair_recv) = refs[:27]
-    sums = refs[27:]
     at = Place(sizes)
-    first_sum = GradSum(at, FIRST_PIECE, FIRST_ORDER, sums[:len(sums) // 2], out_first)
-    last_sum = GradSum(at, LAST_PIECE, LAST_ORDER, sums[len(sums) // 2:], out_last)
+    work = GradSum(at, refs[27:], out_total)
+    grads = work.grads
     nspace = at.nz * NY
     me = at.z * NY + at.y
     rep = at.x * 2 + at.core
@@ -342,9 +325,8 @@
             label = jnp.where(owner_of[j] == member, octslots[j], label)
         lab_out[k] = jnp.full((8, 128), label, jnp.int32)
 
-    first_sum.grads[(SUB_BLOCKS - 1) * SUB_ROWS:] = jnp.zeros(
-        (first_sum.grads.shape[0] - (SUB_BLOCKS - 1) * SUB_ROWS, 128), F32)
-    last_sum.grads[2 * DOWN_ROWS:] = jnp.zeros((last_sum.grads.shape[0] - 2 * DOWN_ROWS, 128), F32)
+    grads[(SUB_BLOCKS - 1) * SUB_ROWS:DOWN_START] = jnp.zeros((SUB_ROWS, 128), F32)
+    grads[USED_ROWS:] = jnp.zeros((grads.shape[0] - USED_ROWS, 128), F32)
 
     def own_planes(bricks):
         for j in bricks:
@@ -491,17 +473,15 @@
             shifted[FINE:2 * FINE, lanes] = middle.astype(BF16)
             shifted[2 * FINE:, lanes] = jnp.where(low, sides[i - 1], sides[i]).astype(BF16)
 
+    part = mul(act_oct[...], ret_half[...], NT)
+    for parity in range(2):
+        start = DOWN_START + parity * DOWN_ROWS
+        grads[start:start + DOWN_ROWS] = part[:, parity * 128:(parity + 1) * 128]
     part = mul(shifted[...], window[...], NT)
     for b in range(SUB_BLOCKS):
         width = min(128, TAPS * FINE - b * 128)
-        first_sum.grads[b * SUB_ROWS:(b + 1) * SUB_ROWS, 0:width] = part[:, b * 128:b * 128 + width]
-    first = first_sum.phases()
-    next(first)
-    part = mul(act_oct[...], ret_half[...], NT)
-    for parity in range(2):
-        last_sum.grads[parity * DOWN_ROWS:(parity + 1) * DOWN_ROWS] = part[:, parity * 128:(parity + 1) * 128]
-    last = last_sum.phases()
-    next(last)
+        grads[b * SUB_ROWS:(b + 1) * SUB_ROWS, 0:width] = part[:, b * 128:b * 128 + width]
+    work.start()
 
     def place_octants():
         for k in range(1, NY):
@@ -520,31 +500,29 @@
             coarse[s] = result[s * COARSE:(s + 1) * COARSE]
 
     save = pltpu.make_async_copy(coarse, out_coarse, load_sem.at[len(loads)])
-    for chunk in (first, last, first, last):
-        next(chunk)
-    place_octants()
-    save.start()
-    for chunk in (first, last, first, last, last, first, first, last, first, last):
-        next(chunk)
+    def while_waiting():
+        place_octants()
+        save.start()
+
+    work.run(while_waiting)
     for copy in started:
         copy.wait_send()
-    first_sum.finish()
-    last_sum.finish()
+    work.finish()
     save.wait()
 
 
-def unpack_kernel(first, last, coarse_in, coarse, grad_sub, grad_down, sub, down, sems):
+def unpack_kernel(total, coarse_in, coarse, grad_sub, grad_down, sub, down, sems):
     copies = [pltpu.make_async_copy(coarse_in, coarse, sems.at[0])]
     copies[0].start()
     for octant in range(8):
-        row = octant % 2 * DOWN_ROWS + octant // 2 * FINE
-        down[octant] = last[row:row + FINE].astype(F32)
+        row = DOWN_START + octant % 2 * DOWN_ROWS + octant // 2 * FINE
+        down[octant] = total[row:row + FINE].astype(F32)
     copies.append(pltpu.make_async_copy(down, grad_down, sems.at[1]))
     copies[-1].start()
 
     def block(b, kx):
         row = b * SUB_ROWS + kx * FINE
-        return first[row:row + FINE].astype(F32)
+        return total[row:row + FINE].astype(F32)
 
     lane = lax.broadcasted_iota(jnp.int32, (FINE, 128), 1)
     for kx in range(3):
@@ -572,16 +550,14 @@
     held = [features[0], occupancy[0], jnp.asarray(padding_matrix()), jnp.asarray(tap_matrix()),
             cotangent[0], jnp.asarray(placing_matrix()), w_sub, jnp.transpose(w_down, (0, 2, 1)),
             jnp.asarray(octant_matrix())]
-    rows = [sum_rows(sizes, piece) for piece in (FIRST_PIECE, LAST_PIECE)]
-    first, last, coarse = pl.pallas_call(
+    total, coarse = pl.pallas_call(
         functools.partial(kernel, sizes),
         out_shape=(
-            jax.ShapeDtypeStruct((rows[0], 128), BF16),
-            jax.ShapeDtypeStruct((rows[1], 128), BF16),
+            jax.ShapeDtypeStruct((2 * sizes[1] * SHARE, 128), BF16),
             jax.ShapeDtypeStruct(cotangent.shape[1:], BF16),
         ),
         in_specs=[smem] * 3 + [hbm] * 9,
-        out_specs=(hbm, hbm, hbm),
+        out_specs=(hbm, hbm),
         scratch_shapes=[v(a.shape, a.dtype) for a in held] + [
             pltpu.SemaphoreType.DMA((10,)),
             v((BRICKS + 1, FINE, 512), BF16),
@@ -610,7 +586,7 @@
             v((2, COARSE, 512), BF16),
             pltpu.SemaphoreType.DMA((2 + 3 * (NY - 1),)),
             pltpu.SemaphoreType.DMA((2 + 3 * (NY - 1),)),
-        ] + sum_scratch(sizes, FIRST_PIECE, FIRST_ORDER) + sum_scratch(sizes, LAST_PIECE, LAST_ORDER),
+        ] + sum_scratch(sizes[1]),
         compiler_params=pltpu.CompilerParams(
             collective_id=0, has_side_effects=True, vmem_limit_bytes=56 * 2**20
         ),
@@ -622,7 +598,7 @@
             jax.ShapeDtypeStruct(w_sub.shape, F32),
             jax.ShapeDtypeStruct((8, FINE, COARSE), F32),
         ),
-        in_specs=[vmem, vmem, vmem],
+        in_specs=[vmem, vmem],
         out_specs=(hbm, hbm, hbm),
         scratch_shapes=[
             v(w_sub.shape, F32),
@@ -630,7 +606,7 @@
             pltpu.SemaphoreType.DMA((5,)),
         ],
         compiler_params=pltpu.CompilerParams(vmem_limit_bytes=56 * 2**20),
-    )(first, last, coarse)
+    )(total, coarse)
     return coarse[None], grad_sub, jnp.transpose(grad_down, (0, 2, 1))
 
 

time: 59.9 us -> 58 us (0.968)
  Pallas kernels: 59.1 us -> 57.2 us
    pallas_call x1, Pallas kernels: 56.6 us -> 54.6 us  [per_device(): pl.pallas_call(functools.partial(kernel, sizes), out_shape=(jax.ShapeDtyp...]
where the time goes in v3:
time: 58 us; the launch traced here: 57.8 us
  Pallas kernels  57.2 us (99%)
  between operations  0.64 us (1%)
    pallas_call x1, Pallas kernels, per_device(): pl.pallas_call(functools.partial(kernel, sizes), out_shape=(jax.ShapeDtyp...  54.6 us
    pallas_call x1, Pallas kernels, per_device(): pl.pallas_call(unpack_kernel, out_shape=(jax.ShapeDtypeStruct(cotangent.s...  2.51 us

profile of v3, /device:TPU:1, one launch (start us, length us, event | category | flops | bytes accessed | tf_op | source)
XLA Modules:
  0.0 57.8 jit_solution(9986766230367956253)
XLA Ops:
  0.6 54.6 %shard_map.139 = (bf16[3072,128]{1,0:T(8,128)(2,1)}, bf16[2,128,512]{2,1,0:T(8,128)(2,1)}) custom-call(s32[4,27]{1,0:T(4,128)} %bitcast.13, s32[4]{0:T(128)} %bitcast.14, s32[4]{0:T(128)} %bitcast.15, bf16[4,96,512]{2,1,0:T(8,128)(2,1)} %bitcast.9, s32[4,512]{1,0:T(4,128)} %bitcast.12, bf16[1152,256]{1,0:T(8,128)(2,1)} %constant.8.clone.refs_2_, ...), custom_call_target="tpu_custom_call" | custom-call | tf_op jit(solution)/shard_map/pallas_call | solution.py:553
  55.3 2.5 %shard_map.140 = (bf16[2,128,512]{2,1,0:T(8,128)(2,1)}, f32[27,96,96]{2,1,0:T(8,128)}, f32[8,96,128]{2,1,0:T(8,128)}) custom-call(bf16[3072,128]{1,0:T(8,128)(2,1)} %get-tuple-element.8.total, bf16[2,128,512]{2,1,0:T(8,128)(2,1)} %get-tuple-element.9.coarse_in), custom_call_target="tpu_custom_call" | custom-call | tf_op jit(solution)/shard_map/pallas_call | solution.py:594

commit v4 on v3

--- a/solution.py
+++ b/solution.py
@@ -167,9 +167,11 @@
                     self.arrive(slots[slot], self.plane_in.at[slot], at.in_plane(-i, -k))
                     summed = summed + self.plane_in[slot].astype(F32)
         self.across_all[c] = summed.astype(BF16)
+        older = list(self.sent)
         slots = self.slots(NY)
         for k in far_first(NY):
             self.send(slots[k], self.across_all.at[c], self.across_all.at[c], at.across_planes(k))
+        self.settle(older)
         for k in near_first(NY):
             self.arrive(slots[k], self.across_all.at[(c - k) % NY], at.across_planes(-k))
         summed = self.across_all[0].astype(F32)
@@ -184,11 +186,14 @@
             return self.total.at[rows_at(start, PIECE)]
 
         self.total[rows_at(core * half + at.x * SHARE + b * PIECE, PIECE)] = summed.astype(BF16)
+        older = list(self.sent)
         slots = self.slots(nx * NY)
         for i in self.far_x:
             for k in far:
                 if i or k:
                     self.send(slots[i * NY + k], piece_of(0, 0), piece_of(0, 0), at.in_plane(i, k))
+        self.settle(older)
+        older = list(self.sent)
         core_slots = self.slots(nx)
         for i in self.near_x:
             for k in near:
@@ -197,13 +202,18 @@
             other = self.total.at[share_of(core, -i)]
             self.send(core_slots[i], other, other, at.across())
             self.save(share_of(core, -i))
+        self.settle(older)
         for i in self.near_x:
             self.arrive(core_slots[i], self.total.at[share_of(1 - core, -i)], at.across())
             self.save(share_of(1 - core, -i))
 
+    def settle(self, copies):
+        for copy in copies:
+            copy.wait_send()
+        self.sent = self.sent[len(copies):]
+
     def finish(self):
-        for copy in self.sent:
-            copy.wait_send()
+        self.settle(list(self.sent))
         for save in self.saved:
             save.wait()
 
@@ -267,10 +277,10 @@
     return hit * table
 
 
-def kernel(sizes, neighbours, owners, octslots, *refs):
-    held, (out_total, out_coarse) = refs[:9], refs[9:11]
-    loaded, refs = refs[11:20], refs[20:]
-    features, occupancy, pad_m, tap_m, cotangent, place_m, w_sub, w_down, oct_m = loaded
+def kernel(sizes, *refs):
+    held, (out_total, out_coarse) = refs[:12], refs[12:14]
+    loaded, refs = refs[14:26], refs[26:]
+    neighbours, owners, octslots, features, occupancy, pad_m, tap_m, cotangent, place_m, w_sub, w_down, oct_m = loaded
     (load_sem, source, upper, lower, gathered, edge, window, active, act_oct, w_cat, w_pair,
      oct_pack, oct_out, oct_in, lab_out, lab_in, table, rep_out, rep_in, returned, ret_half,
      back, shifted, place_in, coarse, pair_send, pair_recv) = refs[:27]
@@ -302,7 +312,7 @@
         copy.start()
         started.append(copy)
 
-    for load in loads[:2]:
+    for load in loads[:5]:
         load.wait()
     occ = occupancy[...].astype(BF16)
     for j in range(BRICKS):
@@ -346,7 +356,7 @@
                     window[t * FINE:(t + 1) * FINE, column:column + 128] = (
                         planes[row:row + FINE, t * 128:(t + 1) * 128])
 
-    for load in loads[2:4]:
+    for load in loads[5:7]:
         load.wait()
     own_planes(range(2))
     pl.semaphore_wait(barrier, len(partners))
@@ -358,7 +368,7 @@
     lab_in[0] = lab_out[0]
 
     own_planes(range(2, BRICKS))
-    for load in loads[4:]:
+    for load in loads[7:]:
         load.wait()
     spread = mul(cotangent[...].reshape(2 * COARSE, 512), place_m[...], NT)
     for s in range(2):
@@ -504,9 +514,8 @@
         place_octants()
         save.start()
 
+    work.sent += started
     work.run(while_waiting)
-    for copy in started:
-        copy.wait_send()
     work.finish()
     save.wait()
 
@@ -544,10 +553,9 @@
 
 def per_device(sizes, features, occupancy, neighbours, owners, octslots, cotangent, w_sub, w_down):
     vmem = pl.BlockSpec(memory_space=pltpu.VMEM)
-    smem = pl.BlockSpec(memory_space=pltpu.SMEM)
     hbm = pl.BlockSpec(memory_space=pl.ANY)
     v = pltpu.VMEM
-    held = [features[0], occupancy[0], jnp.asarray(padding_matrix()), jnp.asarray(tap_matrix()),
+    held = [neighbours[0], owners[0], octslots[0], features[0], occupancy[0], jnp.asarray(padding_matrix()), jnp.asarray(tap_matrix()),
             cotangent[0], jnp.asarray(placing_matrix()), w_sub, jnp.transpose(w_down, (0, 2, 1)),
             jnp.asarray(octant_matrix())]
     total, coarse = pl.pallas_call(
@@ -556,10 +564,11 @@
             jax.ShapeDtypeStruct((2 * sizes[1] * SHARE, 128), BF16),
             jax.ShapeDtypeStruct(cotangent.shape[1:], BF16),
         ),
-        in_specs=[smem] * 3 + [hbm] * 9,
+        in_specs=[hbm] * 12,
         out_specs=(hbm, hbm),
-        scratch_shapes=[v(a.shape, a.dtype) for a in held] + [
-            pltpu.SemaphoreType.DMA((10,)),
+        scratch_shapes=[pltpu.SMEM(a.shape, a.dtype) for a in held[:3]] + [
+            v(a.shape, a.dtype) for a in held[3:]] + [
+            pltpu.SemaphoreType.DMA((13,)),
             v((BRICKS + 1, FINE, 512), BF16),
             v((BRICKS + 1, FINE, 128), BF16),
             v((BRICKS + 1, FINE, 128), BF16),
@@ -590,7 +599,7 @@
         compiler_params=pltpu.CompilerParams(
             collective_id=0, has_side_effects=True, vmem_limit_bytes=56 * 2**20
         ),
-    )(neighbours[0], owners[0], octslots[0], *held)
+    )(*held)
     coarse, grad_sub, grad_down = pl.pallas_call(
         unpack_kernel,
         out_shape=(

time: 58 us -> 57.1 us (0.984)
  Pallas kernels: 57.2 us -> 56.4 us
    pallas_call x1, Pallas kernels: 54.6 us -> 53.9 us  [per_device(): pl.pallas_call(functools.partial(kernel, sizes), out_shape=(jax.ShapeDtyp...]
where the time goes in v4:
time: 57.1 us
  Pallas kernels  56.4 us (99%)
  between operations  0.64 us (1%)
    pallas_call x1, Pallas kernels, per_device(): pl.pallas_call(functools.partial(kernel, sizes), out_shape=(jax.ShapeDtyp...  53.9 us
    pallas_call x1, Pallas kernels, per_device(): pl.pallas_call(unpack_kernel, out_shape=(jax.ShapeDtypeStruct(cotangent.s...  2.51 us

profile of v4, /device:TPU:1, one launch (start us, length us, event | category | flops | bytes accessed | tf_op | source)
XLA Modules:
  0.0 57.1 jit_solution(12625963013857359504)
XLA Ops:
  0.6 53.9 %shard_map.139 = (bf16[3072,128]{1,0:T(8,128)(2,1)}, bf16[2,128,512]{2,1,0:T(8,128)(2,1)}) custom-call(s32[4,27]{1,0:T(4,128)} %bitcast.13, s32[4]{0:T(128)} %bitcast.14, s32[4]{0:T(128)} %bitcast.15, bf16[4,96,512]{2,1,0:T(8,128)(2,1)} %bitcast.9, s32[4,512]{1,0:T(4,128)} %bitcast.12, bf16[1152,256]{1,0:T(8,128)(2,1)} %constant.8.clone.refs_5_, ...), custom_call_target="tpu_custom_call" | custom-call | tf_op jit(solution)/shard_map/pallas_call | solution.py:561
  54.6 2.5 %shard_map.140 = (bf16[2,128,512]{2,1,0:T(8,128)(2,1)}, f32[27,96,96]{2,1,0:T(8,128)}, f32[8,96,128]{2,1,0:T(8,128)}) custom-call(bf16[3072,128]{1,0:T(8,128)(2,1)} %get-tuple-element.8.total, bf16[2,128,512]{2,1,0:T(8,128)(2,1)} %get-tuple-element.9.coarse_in), custom_call_target="tpu_custom_call" | custom-call | tf_op jit(solution)/shard_map/pallas_call | solution.py:603
